TPU v7x, 32 devices: a whole 2x2x4 slice. The times are simulated.
32 devices in a mesh: scene: 8 (over z, x), view: 4 (over y, core).
Axes of the slice: x: 2, y: 2, z: 4, core: 2. Of those that a mesh axis runs over, the one named last changes fastest.
Arguments:
- inputs: bfloat16 [8, 4, 328, 768], P('scene', 'view'), may hold values from -6 to 6
- cameras: int32 [8, 4, 328], P('scene', 'view'), may hold values from 0 to 15
- embedding: float32 [16, 768], replicated, may hold values from -2.5 to 2.5
- scaling: float32 [768], replicated, may hold values from 0.1 to 1.9
- shifting: float32 [768], replicated, may hold values from -2.5 to 2.5
- projector: bfloat16 [768, 2304], replicated, may hold values from -0.3125 to 0.3125
- combiner: bfloat16 [768, 768], replicated, may hold values from -0.625 to 0.625
- baseline: float32 [768], replicated, may hold values from -2.5 to 2.5
- rescaling: float32 [768], replicated, may hold values from 0.1 to 1.9
- reshifting: float32 [768], replicated, may hold values from -2.5 to 2.5
- expander: bfloat16 [768, 1536], replicated, may hold values from -0.21875 to 0.21875
- priming: float32 [1536], replicated, may hold values from -2.5 to 2.5
- squeezer: bfloat16 [1536, 768], replicated, may hold values from -0.15625 to 0.15625
- leveling: float32 [768], replicated, may hold values from -2.5 to 2.5
- cotangent: bfloat16 [8, 4, 328, 768], P('scene', 'view'), may hold values from -6 to 6
Outputs:
- outcome: bfloat16 [8, 4, 328, 768], P('scene', 'view')
- adjoint_inputs: bfloat16 [8, 4, 328, 768], P('scene', 'view')
- adjoint_embedding: float32 [16, 768], replicated
- adjoint_scaling: float32 [768], replicated
- adjoint_shifting: float32 [768], replicated
- adjoint_projector: float32 [768, 2304], replicated
- adjoint_combiner: float32 [768, 768], replicated
- adjoint_baseline: float32 [768], replicated
- adjoint_rescaling: float32 [768], replicated
- adjoint_reshifting: float32 [768], replicated
- adjoint_expander: float32 [768, 1536], replicated
- adjoint_priming: float32 [1536], replicated
- adjoint_squeezer: float32 [1536, 768], replicated
- adjoint_leveling: float32 [768], replicated
All inputs are finite; a program needn't handle non-finite values.
Results may differ from a plain program's by a relative error of at most 0.015.
Values may be sent and summed in bfloat16 or wider, within the bound.
No kernel may reach another device: no remote copies, remote signals or barrier semaphores. Data moves between devices by JAX's collectives and lax.ppermute only.
A program may use at most 192 MiB of HBM per device.

v0:
```python
from functools import partial

import jax
import jax.numpy as jnp
from jax import lax
from jax.sharding import PartitionSpec as P

HEADS = 12
HEAD = 64


def passed_along(value, axis, steps):
    count = lax.axis_size(axis)
    pairs = [(source, (source + steps) % count) for source in range(count)]
    return lax.ppermute(value, axis, pairs)


def layer_norm(values, gain, shift):
    centre = values - jnp.mean(values, axis=-1, keepdims=True)
    spread = jnp.mean(centre * centre, axis=-1, keepdims=True)
    return centre * lax.rsqrt(spread + 1e-05) * gain + shift


def merge_keys(running, queries, key_block, value_block, factor):
    row_max, denominator, accumulated = running
    half_heads = queries.shape[2] // 2
    maxima, totals, weighted = ([], [], [])
    for group_pos in range(2):
        first_head = group_pos * half_heads
        last_head = first_head + half_heads
        scores = (
            jnp.einsum(
                "sqhd,skhd->shqk",
                queries[:, :, first_head:last_head],
                key_block[:, :, first_head:last_head],
                preferred_element_type=jnp.float32,
            )
            * factor
        )
        old_max = row_max[:, first_head:last_head]
        new_max = jnp.maximum(old_max, jnp.max(scores, axis=-1))
        rescale = jnp.exp(old_max - new_max)
        tile_exp = jnp.exp(scores - new_max[..., None])
        totals.append(denominator[:, first_head:last_head] * rescale + jnp.sum(tile_exp, axis=-1))
        update = jnp.einsum(
            "shqk,skhd->sqhd",
            tile_exp.astype(jnp.bfloat16),
            value_block[:, :, first_head:last_head],
            preferred_element_type=jnp.float32,
        )
        weighted.append(
            accumulated[:, :, first_head:last_head] * jnp.transpose(rescale, (0, 2, 1))[..., None]
            + update
        )
        maxima.append(new_max)
    return (
        jnp.concatenate(maxima, axis=1),
        jnp.concatenate(totals, axis=1),
        jnp.concatenate(weighted, axis=2),
    )


def attend(queries, key_local, value_local, factor):
    scenes, patches = (queries.shape[0], queries.shape[1])
    initial = (
        jnp.full((scenes, HEADS, patches), -1e30, jnp.float32),
        jnp.zeros((scenes, HEADS, patches), jnp.float32),
        jnp.zeros(queries.shape, jnp.float32),
    )
    running = initial
    key_block, value_block = (key_local, value_local)
    view_count = lax.axis_size("view")
    for section_pos in range(view_count):
        running = merge_keys(running, queries, key_block, value_block, factor)
        if section_pos + 1 < view_count:
            key_block, value_block = passed_along((key_block, value_block), "view", 1)
    row_max, denominator, accumulated = running
    output_f = accumulated / jnp.transpose(denominator, (0, 2, 1))[..., None]
    return (output_f, row_max + jnp.log(denominator))


def back_block(queries, mix_grad, log_total, delta, key_block, value_block, factor):
    half_heads = queries.shape[2] // 2
    query_parts, key_parts, value_parts = ([], [], [])
    for group_pos in range(2):
        first_head = group_pos * half_heads
        last_head = first_head + half_heads
        query_cut = queries[:, :, first_head:last_head]
        grad_cut = mix_grad[:, :, first_head:last_head]
        key_cut = key_block[:, :, first_head:last_head]
        scores = (
            jnp.einsum("sqhd,skhd->shqk", query_cut, key_cut, preferred_element_type=jnp.float32)
            * factor
        )
        probs = jnp.exp(scores - log_total[:, first_head:last_head, :, None])
        value_parts.append(
            jnp.einsum(
                "shqk,sqhd->skhd",
                probs.astype(jnp.bfloat16),
                grad_cut,
                preferred_element_type=jnp.float32,
            )
        )
        prob_grad = jnp.einsum(
            "sqhd,skhd->shqk",
            grad_cut,
            value_block[:, :, first_head:last_head],
            preferred_element_type=jnp.float32,
        )
        score_grad = (probs * (prob_grad - delta[:, first_head:last_head, :, None])).astype(
            jnp.bfloat16
        )
        query_parts.append(
            jnp.einsum("shqk,skhd->sqhd", score_grad, key_cut, preferred_element_type=jnp.float32)
            * factor
        )
        key_parts.append(
            jnp.einsum("shqk,sqhd->skhd", score_grad, query_cut, preferred_element_type=jnp.float32)
            * factor
        )
    return (
        jnp.concatenate(query_parts, axis=2),
        jnp.concatenate(key_parts, axis=2),
        jnp.concatenate(value_parts, axis=2),
    )


def attend_back(queries, key_local, value_local, mix_grad, log_total, delta, factor):
    view_count = lax.axis_size("view")
    query_grad = jnp.zeros(queries.shape, jnp.float32)
    key_grad = jnp.zeros(queries.shape, jnp.float32)
    value_grad = jnp.zeros(queries.shape, jnp.float32)
    key_block, value_block = (key_local, value_local)
    for section_pos in range(view_count):
        query_part, key_part, value_part = back_block(
            queries, mix_grad, log_total, delta, key_block, value_block, factor
        )
        query_grad = query_grad + query_part
        key_grad = key_grad + key_part
        value_grad = value_grad + value_part
        key_grad, value_grad = (
            passed_along(key_grad.astype(jnp.bfloat16), "view", 1).astype(key_grad.dtype),
            passed_along(value_grad.astype(jnp.bfloat16), "view", 1).astype(value_grad.dtype),
        )
        if section_pos + 1 < view_count:
            key_block, value_block = passed_along((key_block, value_block), "view", 1)
    return (query_grad, key_grad, value_grad)


def forward_pass(inputs, cameras, weights):
    (
        embedding,
        scaling,
        shifting,
        projector,
        combiner,
        baseline,
        rescaling,
        reshifting,
        expander,
        priming,
        squeezer,
        leveling,
    ) = weights
    scenes, patches, model_width = (inputs.shape[0], inputs.shape[2], inputs.shape[3])
    onehot = (
        cameras.reshape(-1)[:, None] == jnp.arange(embedding.shape[0], dtype=jnp.int32)[None, :]
    ).astype(jnp.float32)
    summed = inputs.reshape(-1, model_width).astype(jnp.float32) + jnp.dot(
        onehot, embedding, precision=lax.Precision.HIGHEST
    )
    normed = layer_norm(summed, scaling, shifting).astype(jnp.bfloat16)
    triple = jnp.dot(normed, projector, preferred_element_type=jnp.float32).astype(jnp.bfloat16)
    shaped = triple.reshape(scenes, patches, 3, HEADS, HEAD)
    queries, key_local, value_local = (shaped[:, :, 0], shaped[:, :, 1], shaped[:, :, 2])
    output_f, log_total = attend(queries, key_local, value_local, HEAD ** (-0.5))
    mixed_low = output_f.reshape(-1, model_width).astype(jnp.bfloat16)
    residual = summed + jnp.dot(mixed_low, combiner, preferred_element_type=jnp.float32) + baseline
    second_low = layer_norm(residual, rescaling, reshifting).astype(jnp.bfloat16)
    hidden = jnp.dot(second_low, expander, preferred_element_type=jnp.float32) + priming
    activated = jax.nn.gelu(hidden, approximate=False).astype(jnp.bfloat16)
    outcome = residual + jnp.dot(activated, squeezer, preferred_element_type=jnp.float32) + leveling
    return (
        outcome,
        onehot,
        summed,
        normed,
        queries,
        key_local,
        value_local,
        output_f,
        log_total,
        mixed_low,
        residual,
        second_low,
        hidden,
        activated,
    )


def on_device(
    inputs,
    cameras,
    embedding,
    scaling,
    shifting,
    projector,
    combiner,
    baseline,
    rescaling,
    reshifting,
    expander,
    priming,
    squeezer,
    leveling,
    cotangent,
):
    weights = (
        embedding,
        scaling,
        shifting,
        projector,
        combiner,
        baseline,
        rescaling,
        reshifting,
        expander,
        priming,
        squeezer,
        leveling,
    )
    saved = forward_pass(inputs, cameras, weights)
    outcome = saved[0]
    fenced = lax.optimization_barrier((inputs, cameras, weights))
    saved = forward_pass(fenced[0], fenced[1], fenced[2])
    (
        unused,
        onehot,
        summed,
        normed,
        queries,
        key_local,
        value_local,
        output_f,
        log_total,
        mixed_low,
        residual,
        second_low,
        hidden,
        activated,
    ) = saved
    model_width = inputs.shape[3]
    factor = HEAD ** (-0.5)
    tangent = cotangent.reshape(-1, model_width)
    grad_squeezer = jnp.einsum("tf,td->fd", activated, tangent, preferred_element_type=jnp.float32)
    grad_leveling = jnp.sum(tangent.astype(jnp.float32), axis=0)
    active_grad = jnp.einsum("td,fd->tf", tangent, squeezer, preferred_element_type=jnp.float32)
    gelu_value, gelu_pull = jax.vjp(partial(jax.nn.gelu, approximate=False), hidden)
    hidden_grad = gelu_pull(active_grad)[0].astype(jnp.bfloat16)
    grad_expander = jnp.einsum(
        "td,tf->df", second_low, hidden_grad, preferred_element_type=jnp.float32
    )
    grad_priming = jnp.sum(hidden_grad.astype(jnp.float32), axis=0)
    second_grad = jnp.einsum("tf,df->td", hidden_grad, expander, preferred_element_type=jnp.float32)
    norm_value, norm_pull = jax.vjp(layer_norm, residual, rescaling, reshifting)
    resid_part, grad_rescaling, grad_reshifting = norm_pull(second_grad)
    residual_grad = tangent.astype(jnp.float32) + resid_part
    resid_low = residual_grad.astype(jnp.bfloat16)
    grad_combiner = jnp.einsum(
        "td,te->de", mixed_low, resid_low, preferred_element_type=jnp.float32
    )
    grad_baseline = jnp.sum(resid_low.astype(jnp.float32), axis=0)
    mix_grad = (
        jnp.einsum("te,de->td", resid_low, combiner, preferred_element_type=jnp.float32)
        .astype(jnp.bfloat16)
        .reshape(queries.shape)
    )
    delta = jnp.transpose(jnp.sum(mix_grad.astype(jnp.float32) * output_f, axis=-1), (0, 2, 1))
    query_grad, key_grad, value_grad = attend_back(
        queries, key_local, value_local, mix_grad, log_total, delta, factor
    )
    triple_grad = (
        jnp.stack((query_grad, key_grad, value_grad), axis=2)
        .astype(jnp.bfloat16)
        .reshape(-1, 3 * model_width)
    )
    grad_projector = jnp.einsum(
        "td,te->de", normed, triple_grad, preferred_element_type=jnp.float32
    )
    normed_grad = jnp.einsum(
        "te,de->td", triple_grad, projector, preferred_element_type=jnp.float32
    )
    first_value, first_pull = jax.vjp(layer_norm, summed, scaling, shifting)
    summed_part, grad_scaling, grad_shifting = first_pull(normed_grad)
    summed_grad = residual_grad + summed_part
    grad_embedding = jnp.einsum("tg,td->gd", onehot, summed_grad, precision=lax.Precision.HIGHEST)
    summed_all = lax.psum(
        (
            grad_embedding,
            grad_scaling,
            grad_shifting,
            grad_projector,
            grad_combiner,
            grad_baseline,
            grad_rescaling,
            grad_reshifting,
            grad_expander,
            grad_priming,
            grad_squeezer,
            grad_leveling,
        ),
        ("scene", "view"),
    )
    return (
        outcome.astype(jnp.bfloat16).reshape(inputs.shape),
        summed_grad.astype(jnp.bfloat16).reshape(inputs.shape),
        summed_all[0],
        summed_all[1],
        summed_all[2],
        summed_all[3],
        summed_all[4],
        summed_all[5],
        summed_all[6],
        summed_all[7],
        summed_all[8],
        summed_all[9],
        summed_all[10],
        summed_all[11],
    )


def solution(mesh):
    placed = (
        P("scene", "view", None, None),
        P("scene", "view", None),
        P(),
        P(),
        P(),
        P(),
        P(),
        P(),
        P(),
        P(),
        P(),
        P(),
        P(),
        P(),
        P("scene", "view", None, None),
    )
    return jax.shard_map(
        on_device,
        mesh=mesh,
        in_specs=placed,
        out_specs=(
            P("scene", "view", None, None),
            P("scene", "view", None, None),
            P(),
            P(),
            P(),
            P(),
            P(),
            P(),
            P(),
            P(),
            P(),
            P(),
            P(),
            P(),
        ),
        check_vma=False,
    )
```

profile of v0, /device:TPU:0, one launch (start us, length us, event | category | flops | bytes accessed | tf_op | source)
XLA Modules:
  0.0 663.4 jit_solution(7661643227346551022)
XLA Ops:
  11.1 2.6 convolution_convert_fusion.1
  13.7 3.7 copy.84
  17.4 2.7 slice_bitcast_fusion.3
  20.5 2.6 collective-permute-start.1
  26.0 2.6 convolution_convert_fusion
  28.6 3.7 copy.93
  34.1 4.2 multiply_reduce_fusion.3
  38.3 4.0 multiply_reduce_fusion.7
  45.9 4.1 multiply_reduce_fusion.2
  51.6 17.0 %collective-permute-done.8 = bf16[1,328,12,64]{1,3,2,0:T(8,128)(2,1)S(1)} collective-permute-done((bf16[1,328,12,64]{1,3,2,0:T(8,128)(2,1)S(1)}, bf16[1,328,12,64]{1,3,2,0:T(8,128)(2,1)S(1)}, u32[]{:S(2)}, u32[]{:S(2)}) %collective-permute-start.8) | collective-permute-done | bytes 503840 | tf_op jit(solution)/shard_map/ppermute | solution.py:15
  68.6 6.3 collective-permute-done.9
  76.6 4.6 collective-permute-done.10
  98.4 4.9 fusion.43
  113.8 2.6 fusion.195
  125.8 2.2 fusion.541
  128.1 3.8 fusion.525
  150.0 2.7 collective-permute-done.12
  153.6 5.5 collective-permute-done.17
  159.7 5.7 collective-permute-done.13
  166.2 5.5 collective-permute-done.18
  172.0 6.1 collective-permute-done.14
  180.6 3.8 fusion.348
  184.4 6.3 collective-permute-done.15
  191.1 2.5 multiply_reduce_fusion.18
  197.7 7.0 %fusion.524 = f32[768,2304]{1,0:T(8,128)} fusion(bf16[328,2304]{0,1:T(8,128)(2,1)} %bitcast.998, f32[328,768]{1,0:T(8,128)} %copy-done.20, f32[768]{0:T(1024)S(1)} %copy-done.82, f32[768]{0:T(1024)S(1)} %copy-done.77, f32[328]{0:T(512)S(1)} %copy-done.91, f32[328]{0:T(512)S(1)} %copy-done.87), kind=kOutput, calls=%fused_computation.627 | convolution fusion | flops 1162033152 | bytes 9605696 | tf_op jit(solution)/shard_map/td,te->de/dot_general | solution.py:287
  212.3 4.0 collective-permute-done.4
  240.2 9.7 %fusion.320 = bf16[1,1,328,768]{3,2,1,0:T(8,128)(2,1)} fusion(f32[328,768]{1,0:T(8,128)} %copy-done.49, bf16[1536,768]{1,0:T(8,128)(2,1)} %param.27, bf16[768,1536]{1,0:T(8,128)(2,1)} %param.25, f32[1536]{0:T(1024)} %param.26, f32[768]{0:T(1024)} %param.28, f32[768]{0:T(1024)S(1)} %copy-done.85, f32[768]{0:T(1024)S(1)} %copy-done.80, ...), kind=kOutput, calls=%fused_computation.296 | convolution fusion | flops 1582964736 | bytes 6248000 | tf_op jit(solution)/shard_map/dot_general | solution.py:182
  249.8 72.6 %all-reduce.5.cloned.1.call-done = (f32[16,768]{1,0:T(8,128)}, f32[768]{0:T(1024)}, f32[768]{0:T(1024)}, f32[768]{0:T(1024)}, f32[768]{0:T(1024)}, /*index=5*/f32[768]{0:T(1024)}, f32[1536]{0:T(1024)}, f32[768]{0:T(1024)}) async-done(((f32[16,768]{1,0:T(8,128)}, f32[768]{0:T(1024)}, f32[768]{0:T(1024)}, f32[768]{0:T(1024)}, f32[768]{0:T(1024)}, /*index=5*/f32[768]{0:T(1024)}, f32[1536]{0:T(1024)}, ...) | async-done | bytes 73744 | tf_op jit(solution)/shard_map/psum | solution.py:297
  322.4 314.4 %all-reduce.7.cloned.1.call-done = (f32[768,2304]{1,0:T(8,128)}, f32[768,768]{1,0:T(8,128)}, f32[768,1536]{1,0:T(8,128)}, f32[1536,768]{1,0:T(8,128)}) async-done(((f32[768,2304]{1,0:T(8,128)}, f32[768,768]{1,0:T(8,128)}, f32[768,1536]{1,0:T(8,128)}, f32[1536,768]{1,0:T(8,128)}), (f32[768,2304]{1,0:T(8,128)}, f32[768,768]{1,0:T(8,128)}, f32[768,1536]{1,0:T(8,128)}, ...) | async-done | bytes 18874384 | tf_op jit(solution)/shard_map/psum | solution.py:297
  640.9 6.6 copy.198
  650.7 2.2 copy.203
  653.5 2.2 copy.205
  (404 shorter events, 119.0 us)
Async XLA Ops:
  7.2 315.2 %all-reduce.5.cloned.1.call-start = ((), (), s32[]{:S(2)}) async-start(), calls=%async_computation | async-start | bytes 163840 | tf_op jit(solution)/shard_map/psum | solution.py:297
  20.1 23.7 %collective-permute-start = (bf16[1,328,12,64]{1,3,2,0:T(8,128)(2,1)}, bf16[1,328,12,64]{1,3,2,0:T(8,128)(2,1)}, u32[]{:S(2)}, u32[]{:S(2)}) collective-permute-start(bf16[1,328,12,64]{1,3,2,0:T(8,128)(2,1)} %get-tuple-element.80), channel_id=1, source_target_pairs={{0,1},{1,2},{2,3},{3,0},{4,5},{5,6},{6,7},{7,4},{8,9},{9,10},{10,1... | collective-permute-start | bytes 1511432 | tf_op jit(solution)/shard_map/ppermute | solution.py:15
  20.5 23.4 %collective-permute-start.1 = (bf16[1,328,12,64]{1,3,2,0:T(8,128)(2,1)}, bf16[1,328,12,64]{1,3,2,0:T(8,128)(2,1)}, u32[]{:S(2)}, u32[]{:S(2)}) collective-permute-start(bf16[1,328,12,64]{1,3,2,0:T(8,128)(2,1)} %get-tuple-element.79), channel_id=1, source_target_pairs={{0,1},{1,2},{2,3},{3,0},{4,5},{5,6},{6,7},{7,4},{8,9},{9,10},{10,1... | collective-permute-start | bytes 1511432 | tf_op jit(solution)/shard_map/ppermute | solution.py:15
  34.0 50.3 %copy-start.18 = (bf16[1,328,12,64]{1,3,2,0:T(8,128)(2,1)}, bf16[1,328,12,64]{1,3,2,0:T(8,128)(2,1)S(1)}, u32[]{:S(2)}) copy-start(bf16[1,328,12,64]{1,3,2,0:T(8,128)(2,1)S(1)} %get-tuple-element.78) | copy-start | bytes 1511428
  34.0 54.1 %copy-start.35 = (bf16[1,328,12,64]{1,3,2,0:T(8,128)(2,1)}, bf16[1,328,12,64]{1,3,2,0:T(8,128)(2,1)S(1)}, u32[]{:S(2)}) copy-start(bf16[1,328,12,64]{1,3,2,0:T(8,128)(2,1)S(1)} %get-tuple-element.76) | copy-start | bytes 1511428
  34.0 11.8 %collective-permute-start.6 = (bf16[1,328,12,64]{1,3,2,0:T(8,128)(2,1)S(1)}, bf16[1,328,12,64]{1,3,2,0:T(8,128)(2,1)S(1)}, u32[]{:S(2)}, u32[]{:S(2)}) collective-permute-start(bf16[1,328,12,64]{1,3,2,0:T(8,128)(2,1)S(1)} %get-tuple-element.77), channel_id=1, source_target_pairs={{0,1},{1,2},{2,3},{3,0},{4,5},{5,6},{6,7},{7,4},{8,9},{9,10},{10,1... | collective-permute-start | bytes 1511432 | tf_op jit(solution)/shard_map/ppermute | solution.py:15
  34.1 15.9 %collective-permute-start.7 = (bf16[1,328,12,64]{1,3,2,0:T(8,128)(2,1)S(1)}, bf16[1,328,12,64]{1,3,2,0:T(8,128)(2,1)S(1)}, u32[]{:S(2)}, u32[]{:S(2)}) collective-permute-start(bf16[1,328,12,64]{1,3,2,0:T(8,128)(2,1)S(1)} %get-tuple-element.76), channel_id=1, source_target_pairs={{0,1},{1,2},{2,3},{3,0},{4,5},{5,6},{6,7},{7,4},{8,9},{9,10},{10,1... | collective-permute-start | bytes 1511432 | tf_op jit(solution)/shard_map/ppermute | solution.py:15
  43.0 44.3 %copy-start.13 = (f32[6,328,328]{1,2,0:T(8,128)}, f32[6,328,328]{1,2,0:T(8,128)S(1)}, u32[]{:S(2)}) copy-start(f32[6,328,328]{1,2,0:T(8,128)S(1)} %get-tuple-element.140) | copy-start | bytes 7746052
  43.8 44.3 %copy-start.11 = (f32[6,328,328]{1,2,0:T(8,128)}, f32[6,328,328]{1,2,0:T(8,128)S(1)}, u32[]{:S(2)}) copy-start(f32[6,328,328]{1,2,0:T(8,128)S(1)} %get-tuple-element.148) | copy-start | bytes 7746052
  43.8 162.8 %collective-permute-start.2 = (bf16[1,328,12,64]{1,3,2,0:T(8,128)(2,1)}, bf16[1,328,12,64]{1,3,2,0:T(8,128)(2,1)}, u32[]{:S(2)}, u32[]{:S(2)}) collective-permute-start(bf16[1,328,12,64]{1,3,2,0:T(8,128)(2,1)} %collective-permute-done), channel_id=1, source_target_pairs={{0,1},{1,2},{2,3},{3,0},{4,5},{5,6},{6,7},{7,4},{8,9},{9,10},{10,1... | collective-permute-start | bytes 1511432 | tf_op jit(solution)/shard_map/ppermute | solution.py:15
  43.9 162.8 %collective-permute-start.3 = (bf16[1,328,12,64]{1,3,2,0:T(8,128)(2,1)}, bf16[1,328,12,64]{1,3,2,0:T(8,128)(2,1)}, u32[]{:S(2)}, u32[]{:S(2)}) collective-permute-start(bf16[1,328,12,64]{1,3,2,0:T(8,128)(2,1)} %collective-permute-done.1), channel_id=1, source_target_pairs={{0,1},{1,2},{2,3},{3,0},{4,5},{5,6},{6,7},{7,4},{8,9},{9,10},{10,1... | collective-permute-start | bytes 1511432 | tf_op jit(solution)/shard_map/ppermute | solution.py:15
  45.8 22.8 %collective-permute-start.8 = (bf16[1,328,12,64]{1,3,2,0:T(8,128)(2,1)S(1)}, bf16[1,328,12,64]{1,3,2,0:T(8,128)(2,1)S(1)}, u32[]{:S(2)}, u32[]{:S(2)}) collective-permute-start(bf16[1,328,12,64]{1,3,2,0:T(8,128)(2,1)S(1)} %collective-permute-done.6), channel_id=1, source_target_pairs={{0,1},{1,2},{2,3},{3,0},{4,5},{5,6},{6,7},{7,4},{8,9},{9,10},{10,1... | collective-permute-start | bytes 1511432 | tf_op jit(solution)/shard_map/ppermute | solution.py:15
  50.0 41.7 %copy-start.50 = (bf16[1,328,12,64]{1,3,2,0:T(8,128)(2,1)}, bf16[1,328,12,64]{1,3,2,0:T(8,128)(2,1)S(1)}, u32[]{:S(2)}) copy-start(bf16[1,328,12,64]{1,3,2,0:T(8,128)(2,1)S(1)} %collective-permute-done.7) | copy-start | bytes 1511428
  50.0 24.9 %collective-permute-start.9 = (bf16[1,328,12,64]{1,3,2,0:T(8,128)(2,1)S(1)}, bf16[1,328,12,64]{1,3,2,0:T(8,128)(2,1)S(1)}, u32[]{:S(2)}, u32[]{:S(2)}) collective-permute-start(bf16[1,328,12,64]{1,3,2,0:T(8,128)(2,1)S(1)} %collective-permute-done.7), channel_id=1, source_target_pairs={{0,1},{1,2},{2,3},{3,0},{4,5},{5,6},{6,7},{7,4},{8,9},{9,10},{10,1... | collective-permute-start | bytes 1511432 | tf_op jit(solution)/shard_map/ppermute | solution.py:15
  50.9 38.0 %copy-start.7 = (f32[6,328,328]{1,2,0:T(8,128)}, f32[6,328,328]{1,2,0:T(8,128)S(1)}, u32[]{:S(2)}) copy-start(f32[6,328,328]{1,2,0:T(8,128)S(1)} %get-tuple-element.138) | copy-start | bytes 7746052
  51.6 40.1 %copy-start.9 = (f32[6,328,328]{1,2,0:T(8,128)}, f32[6,328,328]{1,2,0:T(8,128)S(1)}, u32[]{:S(2)}) copy-start(f32[6,328,328]{1,2,0:T(8,128)S(1)} %get-tuple-element.146) | copy-start | bytes 7746052
  68.6 12.6 %collective-permute-start.10 = (bf16[1,328,12,64]{1,3,2,0:T(8,128)(2,1)S(1)}, bf16[1,328,12,64]{1,3,2,0:T(8,128)(2,1)S(1)}, u32[]{:S(2)}, u32[]{:S(2)}) collective-permute-start(bf16[1,328,12,64]{1,3,2,0:T(8,128)(2,1)S(1)} %collective-permute-done.8), channel_id=1, source_target_pairs={{0,1},{1,2},{2,3},{3,0},{4,5},{5,6},{6,7},{7,4},{8,9},{9,10},{10,1... | collective-permute-start | bytes 1511432 | tf_op jit(solution)/shard_map/ppermute | solution.py:15
  74.9 17.5 %copy-start.52 = (bf16[1,328,12,64]{1,3,2,0:T(8,128)(2,1)}, bf16[1,328,12,64]{1,3,2,0:T(8,128)(2,1)S(1)}, u32[]{:S(2)}) copy-start(bf16[1,328,12,64]{1,3,2,0:T(8,128)(2,1)S(1)} %collective-permute-done.9) | copy-start | bytes 1511428
  74.9 16.0 %collective-permute-start.11 = (bf16[1,328,12,64]{1,3,2,0:T(8,128)(2,1)S(1)}, bf16[1,328,12,64]{1,3,2,0:T(8,128)(2,1)S(1)}, u32[]{:S(2)}, u32[]{:S(2)}) collective-permute-start(bf16[1,328,12,64]{1,3,2,0:T(8,128)(2,1)S(1)} %collective-permute-done.9), channel_id=1, source_target_pairs={{0,1},{1,2},{2,3},{3,0},{4,5},{5,6},{6,7},{7,4},{8,9},{9,10},{10,1... | collective-permute-start | bytes 1511432 | tf_op jit(solution)/shard_map/ppermute | solution.py:15
  75.9 14.3 %copy-start.15 = (f32[6,328,328]{1,2,0:T(8,128)}, f32[6,328,328]{1,2,0:T(8,128)S(1)}, u32[]{:S(2)}) copy-start(f32[6,328,328]{1,2,0:T(8,128)S(1)} %get-tuple-element.136) | copy-start | bytes 7746052
  76.6 15.8 %copy-start.5 = (f32[6,328,328]{1,2,0:T(8,128)}, f32[6,328,328]{1,2,0:T(8,128)S(1)}, u32[]{:S(2)}) copy-start(f32[6,328,328]{1,2,0:T(8,128)S(1)} %get-tuple-element.144) | copy-start | bytes 7746052
  132.0 17.5 %collective-permute-start.16 = (bf16[1,328,12,64]{1,3,2,0:T(8,128)(2,1)S(1)}, bf16[1,328,12,64]{1,3,2,0:T(8,128)(2,1)S(1)}, u32[]{:S(2)}, u32[]{:S(2)}) collective-permute-start(bf16[1,328,12,64]{1,3,2,0:T(8,128)(2,1)S(1)} %pad_maximum_fusion.4), channel_id=1, source_target_pairs={{0,1},{1,2},{2,3},{3,0},{4,5},{5,6},{6,7},{7,4},{8,9},{9,10},{10,1... | collective-permute-start | bytes 1511432 | tf_op jit(solution)/shard_map/ppermute | solution.py:15
  143.4 9.4 %collective-permute-start.12 = (bf16[1,328,12,64]{1,3,2,0:T(8,128)(2,1)S(1)}, bf16[1,328,12,64]{1,3,2,0:T(8,128)(2,1)S(1)}, u32[]{:S(2)}, u32[]{:S(2)}) collective-permute-start(bf16[1,328,12,64]{1,3,2,0:T(8,128)(2,1)S(1)} %pad_maximum_fusion.3), channel_id=1, source_target_pairs={{0,1},{1,2},{2,3},{3,0},{4,5},{5,6},{6,7},{7,4},{8,9},{9,10},{10,1... | collective-permute-start | bytes 1511432 | tf_op jit(solution)/shard_map/ppermute | solution.py:15
  149.7 9.4 %collective-permute-start.17 = (bf16[1,328,12,64]{1,3,2,0:T(8,128)(2,1)S(1)}, bf16[1,328,12,64]{1,3,2,0:T(8,128)(2,1)S(1)}, u32[]{:S(2)}, u32[]{:S(2)}) collective-permute-start(bf16[1,328,12,64]{1,3,2,0:T(8,128)(2,1)S(1)} %fusion.335), channel_id=1, source_target_pairs={{0,1},{1,2},{2,3},{3,0},{4,5},{5,6},{6,7},{7,4},{8,9},{9,10},{10,1... | collective-permute-start | bytes 1511432 | tf_op jit(solution)/shard_map/ppermute | solution.py:15
  152.9 12.5 %collective-permute-start.13 = (bf16[1,328,12,64]{1,3,2,0:T(8,128)(2,1)S(1)}, bf16[1,328,12,64]{1,3,2,0:T(8,128)(2,1)S(1)}, u32[]{:S(2)}, u32[]{:S(2)}) collective-permute-start(bf16[1,328,12,64]{1,3,2,0:T(8,128)(2,1)S(1)} %fusion.332), channel_id=1, source_target_pairs={{0,1},{1,2},{2,3},{3,0},{4,5},{5,6},{6,7},{7,4},{8,9},{9,10},{10,1... | collective-permute-start | bytes 1511432 | tf_op jit(solution)/shard_map/ppermute | solution.py:15
  159.3 12.4 %collective-permute-start.18 = (bf16[1,328,12,64]{1,3,2,0:T(8,128)(2,1)S(1)}, bf16[1,328,12,64]{1,3,2,0:T(8,128)(2,1)S(1)}, u32[]{:S(2)}, u32[]{:S(2)}) collective-permute-start(bf16[1,328,12,64]{1,3,2,0:T(8,128)(2,1)S(1)} %fusion.336), channel_id=1, source_target_pairs={{0,1},{1,2},{2,3},{3,0},{4,5},{5,6},{6,7},{7,4},{8,9},{9,10},{10,1... | collective-permute-start | bytes 1511432 | tf_op jit(solution)/shard_map/ppermute | solution.py:15
  165.5 12.5 %collective-permute-start.14 = (bf16[1,328,12,64]{1,3,2,0:T(8,128)(2,1)S(1)}, bf16[1,328,12,64]{1,3,2,0:T(8,128)(2,1)S(1)}, u32[]{:S(2)}, u32[]{:S(2)}) collective-permute-start(bf16[1,328,12,64]{1,3,2,0:T(8,128)(2,1)S(1)} %fusion.333), channel_id=1, source_target_pairs={{0,1},{1,2},{2,3},{3,0},{4,5},{5,6},{6,7},{7,4},{8,9},{9,10},{10,1... | collective-permute-start | bytes 1511432 | tf_op jit(solution)/shard_map/ppermute | solution.py:15
  171.9 12.5 %collective-permute-start.19 = (bf16[1,328,12,64]{1,3,2,0:T(8,128)(2,1)S(1)}, bf16[1,328,12,64]{1,3,2,0:T(8,128)(2,1)S(1)}, u32[]{:S(2)}, u32[]{:S(2)}) collective-permute-start(bf16[1,328,12,64]{1,3,2,0:T(8,128)(2,1)S(1)} %fusion.337), channel_id=1, source_target_pairs={{0,1},{1,2},{2,3},{3,0},{4,5},{5,6},{6,7},{7,4},{8,9},{9,10},{10,1... | collective-permute-start | bytes 1511432 | tf_op jit(solution)/shard_map/ppermute | solution.py:15
  178.2 12.4 %collective-permute-start.15 = (bf16[1,328,12,64]{1,3,2,0:T(8,128)(2,1)S(1)}, bf16[1,328,12,64]{1,3,2,0:T(8,128)(2,1)S(1)}, u32[]{:S(2)}, u32[]{:S(2)}) collective-permute-start(bf16[1,328,12,64]{1,3,2,0:T(8,128)(2,1)S(1)} %fusion.334), channel_id=1, source_target_pairs={{0,1},{1,2},{2,3},{3,0},{4,5},{5,6},{6,7},{7,4},{8,9},{9,10},{10,1... | collective-permute-start | bytes 1511432 | tf_op jit(solution)/shard_map/ppermute | solution.py:15
  197.6 439.2 %all-reduce.7.cloned.1.call-start = ((), (), s32[]{:S(2)}) async-start(), calls=%async_computation.1 | async-start | bytes 37748736 | tf_op jit(solution)/shard_map/psum | solution.py:297
  206.6 9.7 %collective-permute-start.4 = (bf16[1,328,12,64]{1,3,2,0:T(8,128)(2,1)}, bf16[1,328,12,64]{1,3,2,0:T(8,128)(2,1)S(1)}, u32[]{:S(2)}, u32[]{:S(2)}) collective-permute-start(bf16[1,328,12,64]{1,3,2,0:T(8,128)(2,1)} %collective-permute-done.2), channel_id=1, source_target_pairs={{0,1},{1,2},{2,3},{3,0},{4,5},{5,6},{6,7},{7,4},{8,9},{9,10},{10,1... | collective-permute-start | bytes 1511432 | tf_op jit(solution)/shard_map/ppermute | solution.py:15
  206.7 24.9 %collective-permute-start.5 = (bf16[1,328,12,64]{1,3,2,0:T(8,128)(2,1)}, bf16[1,328,12,64]{1,3,2,0:T(8,128)(2,1)S(1)}, u32[]{:S(2)}, u32[]{:S(2)}) collective-permute-start(bf16[1,328,12,64]{1,3,2,0:T(8,128)(2,1)} %collective-permute-done.3), channel_id=1, source_target_pairs={{0,1},{1,2},{2,3},{3,0},{4,5},{5,6},{6,7},{7,4},{8,9},{9,10},{10,1... | collective-permute-start | bytes 1511432 | tf_op jit(solution)/shard_map/ppermute | solution.py:15
  (105 other events, 322.8 us)
Sparse Core Ops, SparseCore 0:
  197.7 124.6 all-reduce.4
  330.0 306.7 all-reduce.6
where the time goes:
time: 673 us; the launch traced here: 663 us
  waiting for transfers between devices  451 us (67%)
  matrix products  116 us (17%)
  local copies, waits for them, and re-layouts  53.1 us (8%)
  other arithmetic  16.9 us (3%)
  between operations  16.1 us (2%)
  starting transfers between devices  10.9 us (2%)
    psum x2, waiting for transfers between devices, on_device(): lax.psum((grad_embedding, grad_scaling, grad_shifting, grad_projector, gr...  387 us
    ppermute x20, waiting for transfers between devices, passed_along(): return lax.ppermute(value, axis, pairs)  63.8 us
    unnamed x242, local copies, waits for them, and re-layouts  38.6 us
    dot_general x16, matrix products, merge_keys(): jnp.einsum('sqhd,skhd->shqk', queries[:, :, first_head:last_head], key_bl...  24.9 us
    dot_general x16, matrix products, merge_keys(): jnp.einsum('shqk,skhd->sqhd', tile_exp.astype(jnp.bfloat16), value_block[...  17.9 us
  transfers between devices with their start and end apart: 22, of which 12 were waited for; matrix products, arithmetic and copies ran while one was open for 20% of the time, Pallas kernels for 0%

commit v1 on v0

v1 whole, which is shorter than its diff:
```python
import jax
import jax.numpy as jnp
from jax import lax
from jax.sharding import PartitionSpec as P

HEADS = 12
HEAD = 64
BF = jnp.bfloat16
F32 = jnp.float32
BOTH = ("scene", "view")


def swap(value, axis, mask):
    count = lax.axis_size(axis)
    return lax.ppermute(value, axis, [(i, i ^ mask) for i in range(count)])


def swap_by_core(value, masks):
    scenes, views = lax.axis_size("scene"), lax.axis_size("view")
    pairs = []
    for s in range(scenes):
        for v in range(views):
            ds, dv = masks[v % 2]
            pairs.append((s * views + v, (s ^ ds) * views + (v ^ dv)))
    return lax.ppermute(value, BOTH, pairs)


def side_of(masks):
    scene, view = lax.axis_index("scene"), lax.axis_index("view")
    bits = []
    for ds, dv in masks:
        bits.append(((scene & ds) + (view & dv) > 0).astype(jnp.int32))
    return jnp.where(view % 2 == 0, bits[0], bits[1])


CORE = ((0, 1), (0, 1))
X, Y, Z1, Z2 = (1, 0), (0, 2), (2, 0), (4, 0)
FULL = (CORE, (X, Z1), (Y, X), (Z1, Y), (Z2, Z2))
SCENE = ((X, Z1), (Z1, X), (Z2, Z2))
VIEW = ((Y, Y), CORE)


def reduce_scatter(value, stages):
    for masks in stages:
        half = value.shape[0] // 2
        side = side_of(masks)
        send = lax.dynamic_slice_in_dim(value, (1 - side) * half, half, 0)
        keep = lax.dynamic_slice_in_dim(value, side * half, half, 0)
        got = swap_by_core(send, masks)
        value = (keep.astype(F32) + got.astype(F32)).astype(BF)
    bit = 8
    while bit < lax.axis_size("scene"):
        value = (value.astype(F32) + swap(value, "scene", bit).astype(F32)).astype(BF)
        bit *= 2
    return value


def all_gather(value, stages):
    for masks in reversed(stages):
        side = side_of(masks)
        got = swap_by_core(value, masks)
        value = jnp.concatenate(
            [jnp.where(side == 0, value, got), jnp.where(side == 0, got, value)], 0
        )
    return value


def by_view(blocks, me):
    a, b, c, d = blocks
    one = (me & 1) == 1
    a, b = jnp.where(one, b, a), jnp.where(one, a, b)
    c, d = jnp.where(one, d, c), jnp.where(one, c, d)
    two = (me & 2) == 2
    a, c = jnp.where(two, c, a), jnp.where(two, a, c)
    b, d = jnp.where(two, d, b), jnp.where(two, b, d)
    return a, b, c, d


def normalise(values):
    centre = values - jnp.mean(values, axis=-1, keepdims=True)
    rstd = lax.rsqrt(jnp.mean(centre * centre, axis=-1, keepdims=True) + 1e-05)
    return centre * rstd, rstd


def norm_back(grad, unit, rstd):
    return (
        grad
        - jnp.mean(grad, axis=-1, keepdims=True)
        - unit * jnp.mean(grad * unit, axis=-1, keepdims=True)
    ) * rstd


def dot(a, b):
    return jnp.dot(a, b, preferred_element_type=F32)


def tdot(a, b):
    return lax.dot_general(a, b, (((0,), (0,)), ((), ())), preferred_element_type=F32)


def dott(a, b):
    return lax.dot_general(a, b, (((1,), (1,)), ((), ())), preferred_element_type=F32)


def on_device(
    inputs,
    cameras,
    embedding,
    scaling,
    shifting,
    projector,
    combiner,
    baseline,
    rescaling,
    reshifting,
    expander,
    priming,
    squeezer,
    leveling,
    cotangent,
):
    me = lax.axis_index("view")
    patches, width = inputs.shape[2], inputs.shape[3]
    mine = HEADS // 4 * HEAD
    tangent = cotangent.reshape(patches, width)
    x0 = inputs.reshape(patches, width)
    c0 = cameras.reshape(patches)
    x2, c2 = swap(x0, "view", 2), swap(c0, "view", 2)
    x1, c1 = swap(x0, "view", 1), swap(c0, "view", 1)
    x3, c3 = swap(x2, "view", 1), swap(c2, "view", 1)
    tokens = jnp.concatenate([x0, x1, x2, x3], 0)
    groups = jnp.concatenate([c0, c1, c2, c3], 0)
    onehot = (groups[:, None] == jnp.arange(embedding.shape[0])[None, :]).astype(F32)
    summed = tokens.astype(F32) + jnp.dot(onehot, embedding, precision=lax.Precision.HIGHEST)
    unit1, rstd1 = normalise(summed)
    normed = (unit1 * scaling + shifting).astype(BF)
    weight = jnp.concatenate(
        [
            lax.dynamic_slice_in_dim(projector, part * width + me * mine, mine, 1)
            for part in range(3)
        ],
        1,
    )
    triple = dot(normed, weight).astype(BF)
    total = 4 * patches
    q = triple[:, :mine].reshape(total, 3, HEAD) * BF(HEAD**-0.5)
    k = triple[:, mine : 2 * mine].reshape(total, 3, HEAD)
    v = triple[:, 2 * mine :].reshape(total, 3, HEAD)
    scores = jnp.einsum("qhd,khd->hqk", q, k, preferred_element_type=F32)
    top = jnp.max(scores, -1, keepdims=True)
    expo = jnp.exp(scores - top)
    denom = jnp.sum(expo, -1)
    expo = expo.astype(BF)
    inverse = (1.0 / denom).T[:, :, None]
    mixture = jnp.einsum("hqk,khd->qhd", expo, v, preferred_element_type=F32) * inverse
    mixed_mine = mixture.reshape(total, mine).astype(BF)
    mixed_rel = [mixed_mine[r * patches : (r + 1) * patches] for r in range(4)]
    mixed_rel = [mixed_rel[0]] + [swap(mixed_rel[r], "view", r) for r in (1, 2, 3)]
    mixed = jnp.concatenate(by_view(mixed_rel, me), 1)
    residual = summed[:patches] + dot(mixed, combiner) + baseline
    unit2, rstd2 = normalise(residual)
    second = (unit2 * rescaling + reshifting).astype(BF)
    hidden = dot(second, expander) + priming
    phi = 0.5 * (1.0 + lax.erf(hidden * (2.0**-0.5)))
    density = jnp.exp(-0.5 * hidden * hidden) * ((2.0 * jnp.pi) ** -0.5)
    active = (hidden * phi).astype(BF)
    outcome = residual + dot(active, squeezer) + leveling
    hidden_grad = (dott(tangent, squeezer) * (phi + hidden * density)).astype(BF)
    second_grad = dott(hidden_grad, expander)
    tangent_f = tangent.astype(F32)
    residual_grad = tangent_f + norm_back(second_grad * rescaling, unit2, rstd2)
    resid_low = residual_grad.astype(BF)
    mix_grad = dott(resid_low, combiner).astype(BF)
    mix_rel = by_view([mix_grad[:, r * mine : (r + 1) * mine] for r in range(4)], me)
    mix_rel = [mix_rel[0]] + [swap(mix_rel[r], "view", r) for r in (1, 2, 3)]

    grad_squeezer = tdot(active, tangent).astype(BF)
    grad_expander = tdot(second, hidden_grad).astype(BF)
    grad_combiner = tdot(mixed, resid_low).astype(BF)
    rows = [
        jnp.sum(tangent_f, 0),
        jnp.sum(resid_low.astype(F32), 0),
        jnp.sum(second_grad * unit2, 0),
        jnp.sum(second_grad, 0),
        jnp.sum(hidden_grad.astype(F32), 0).reshape(2, width),
    ]
    rows = jnp.concatenate([r.reshape(-1, width) for r in rows], 0)
    rows = jnp.concatenate([rows, jnp.zeros((32 - rows.shape[0], width), F32)], 0).astype(BF)
    big = jnp.concatenate([grad_squeezer, grad_expander.reshape(-1, width), grad_combiner, rows], 0)
    big = reduce_scatter(big, FULL)
    big = all_gather(big, FULL)

    grad_out = jnp.concatenate(mix_rel, 0).reshape(total, 3, HEAD)
    delta = jnp.sum(grad_out.astype(F32) * mixture, -1).T[:, :, None]
    probs = expo.astype(F32) * (1.0 / denom)[:, :, None]
    prob_grad = jnp.einsum("qhd,khd->hqk", grad_out, v, preferred_element_type=F32)
    score_grad = (probs * (prob_grad - delta)).astype(BF)
    v_grad = jnp.einsum("hqk,qhd->khd", probs.astype(BF), grad_out, preferred_element_type=F32)
    q_grad = jnp.einsum("hqk,khd->qhd", score_grad, k, preferred_element_type=F32) * HEAD**-0.5
    k_grad = jnp.einsum("hqk,qhd->khd", score_grad, q, preferred_element_type=F32)
    triple_grad = jnp.concatenate(
        [g.reshape(total, mine) for g in (q_grad, k_grad, v_grad)], 1
    ).astype(BF)
    grad_weight = tdot(normed, triple_grad).astype(BF)
    normed_grad = dott(triple_grad, weight)
    summed_part = norm_back(normed_grad * scaling, unit1, rstd1)
    onehot_sum = lax.dot_general(
        onehot, summed_part, (((0,), (0,)), ((), ())), precision=lax.Precision.HIGHEST
    ) + lax.dot_general(
        onehot[:patches], residual_grad, (((0,), (0,)), ((), ())), precision=lax.Precision.HIGHEST
    )
    tail = jnp.concatenate(
        [onehot_sum, jnp.sum(normed_grad * unit1, 0)[None], jnp.sum(normed_grad, 0)[None]], 0
    )
    tail = tail.astype(BF).reshape(24, 3 * mine)
    late = jnp.concatenate([grad_weight, tail], 0)
    late = reduce_scatter(late, SCENE)
    late = all_gather(late, VIEW + SCENE)

    part = [summed_part[r * patches : (r + 1) * patches] for r in range(4)]
    keep = part[0] + swap(part[1].astype(BF), "view", 1).astype(F32)
    send = part[2] + swap(part[3].astype(BF), "view", 1).astype(F32)
    inputs_grad = residual_grad + keep + swap(send.astype(BF), "view", 2).astype(F32)

    late = late.reshape(2, 2, width + 24, 3 * mine).astype(F32)
    late = late.transpose(1, 0, 2, 3).reshape(4, width + 24, 3 * mine) if False else late.reshape(4, width + 24, 3 * mine)
    small = jnp.sum(late[:, width:], 0).reshape(18, width)
    grad_projector = (
        late[:, :width].reshape(4, width, 3, mine).transpose(1, 2, 0, 3).reshape(width, 3 * width)
    )
    big = big.astype(F32)
    hid = grad_squeezer.shape[0]
    at = 2 * hid + width
    return (
        outcome.astype(BF).reshape(inputs.shape),
        inputs_grad.astype(BF).reshape(inputs.shape),
        small[:16],
        small[16],
        small[17],
        grad_projector,
        big[2 * hid : at],
        big[at + 1],
        big[at + 2],
        big[at + 3],
        big[hid : 2 * hid].reshape(width, hid),
        big[at + 4 : at + 6].reshape(hid),
        big[:hid],
        big[at],
    )


def solution(mesh):
    tokens = P("scene", "view", None, None)
    placed = (tokens, P("scene", "view", None)) + (P(),) * 12 + (tokens,)
    return jax.shard_map(
        on_device,
        mesh=mesh,
        in_specs=placed,
        out_specs=(tokens, tokens) + (P(),) * 12,
        check_vma=False,
    )
```

time: 673 us -> 431 us (0.64)
  waiting for transfers between devices: 451 us -> 112 us
  local copies, waits for them, and re-layouts: 53.1 us -> 130 us
  other arithmetic: 16.9 us -> 58.6 us
  matrix products: 116 us -> 89.6 us
  starting transfers between devices: 10.9 us -> 32.1 us
  between operations: 16.1 us -> 1.69 us
    psum x2 -> x0, waiting for transfers between devices: 387 us -> none  [on_device(): lax.psum((grad_embedding, grad_scaling, grad_shifting, grad_projector, gr...]
    ppermute x20 -> x33, waiting for transfers between devices: 63.8 us -> 112 us  [the longest x18 61.8 us: swap_by_core(): return lax.ppermute(value, BOTH, pairs)]
    slice x0 -> x12, local copies, waits for them, and re-layouts: none -> 39.3 us  [the longest x2 15.6 us: on_device(): late[:, :width].reshape(4, width, 3, mine).transpose(1, 2, 0, 3)]
    dot_general x81 -> x20, matrix products: 116 us -> 79.7 us  [the longest x1 14.3 us: on_device(): jnp.einsum('qhd,khd->hqk', grad_out, v, preferred_element_type=F32)]
    concatenate x0 -> x5, local copies, waits for them, and re-layouts: none -> 32.8 us  [the longest x1 28.8 us: on_device(): jnp.concatenate([grad_squeezer, grad_expander.reshape(-1, width), grad_co...]
    unnamed x242 -> x91, local copies, waits for them, and re-layouts: 38.6 us -> 15.8 us
    ppermute x20 -> x33, starting transfers between devices: 10.8 us -> 32.1 us  [the longest x18 22.2 us: swap_by_core(): return lax.ppermute(value, BOTH, pairs)]
    convert_element_type x8 -> x12, other arithmetic: 1.21 us -> 20.7 us  [the longest x8 8.32 us: reduce_scatter(): value = (keep.astype(F32) + got.astype(F32)).astype(BF)]
  transfers between devices with their start and end apart: 22 -> 33, of which waited for: 12 -> 15; matrix products, arithmetic and copies ran while one was open for 20% -> 43% of each run, Pallas kernels for 0% -> 0%
where the time goes in v1:
time: 431 us; the launch traced here: 423 us
  local copies, waits for them, and re-layouts  130 us (30%)
  waiting for transfers between devices  112 us (26%)
  matrix products  89.6 us (21%)
  other arithmetic  58.6 us (14%)
  starting transfers between devices  32.1 us (7%)
    ppermute x18, waiting for transfers between devices, swap_by_core(): return lax.ppermute(value, BOTH, pairs)  61.8 us
    ppermute x15, waiting for transfers between devices, swap(): return lax.ppermute(value, axis, [(i, i ^ mask) for i in range(count)])  49.8 us
    concatenate x1, local copies, waits for them, and re-layouts, on_device(): jnp.concatenate([grad_squeezer, grad_expander.reshape(-1, width), grad_co...  28.8 us
    ppermute x18, starting transfers between devices, swap_by_core(): return lax.ppermute(value, BOTH, pairs)  22.2 us
    unnamed x91, local copies, waits for them, and re-layouts  15.8 us
    slice x2, local copies, waits for them, and re-layouts, on_device(): late[:, :width].reshape(4, width, 3, mine).transpose(1, 2, 0, 3)  15.6 us
    dot_general x1, matrix products, on_device(): jnp.einsum('qhd,khd->hqk', grad_out, v, preferred_element_type=F32)  14.3 us
    select_n x10, other arithmetic, all_gather(): jnp.where(side == 0, value, got)  13.2 us
  transfers between devices with their start and end apart: 33, of which 15 were waited for; matrix products, arithmetic and copies ran while one was open for 43% of the time, Pallas kernels for 0%

profile of v1, /device:TPU:0, one launch (start us, length us, event | category | flops | bytes accessed | tf_op | source)
XLA Modules:
  0.0 423.2 jit_solution(7567199935735776353)
XLA Ops:
  5.1 10.4 %collective-permute-done.1 = bf16[328,768]{1,0:T(8,128)(2,1)} collective-permute-done((bf16[328,768]{1,0:T(8,128)(2,1)}, bf16[328,768]{1,0:T(8,128)(2,1)}, u32[]{:S(2)}, u32[]{:S(2)}) %collective-permute-start.1) | collective-permute-done | bytes 503840 | tf_op jit(solution)/shard_map/ppermute | solution.py:15
  22.1 3.5 fusion.59
  30.4 9.9 %exponential_reduce_fusion = (f32[3,1312]{1,0:T(4,128)S(1)}, f32[3,1312,1312]{1,2,0:T(8,128)}) fusion(bf16[1312,3,64]{0,2,1:T(8,128)(2,1)S(1)} %bitcast.80, bf16[1312,3,64]{0,2,1:T(8,128)(2,1)S(1)} %bitcast.76), kind=kOutput, calls=%fused_computation.5 | convolution fusion | flops 671325440 | bytes 21679488 | tf_op jit(solution)/shard_map/sub | solution.py:151
  40.4 9.1 %fusion.60 = (bf16[1312,3,64]{0,2,1:T(8,128)(2,1)}, f32[1312,3,64]{0,2,1:T(8,128)}) fusion(f32[1312,3]{0,1:T(4,128)S(1)} %fusion.94, bf16[1312,3,64]{0,2,1:T(8,128)(2,1)} %bitcast.89, bf16[1312,3,64]{0,2,1:T(8,128)(2,1)S(1)} %bitcast.81, bf16[1312,3,64]{0,2,1:T(8,128)(2,1)S(1)} %bitcast.77), kind=kOutput, calls=%fused_computation.180 | convolution fusion | flops 1332829312 | bytes 3038592 | tf_op jit(solution)/shard_map/hqk,khd->qhd/dot_general | solution.py:155
  63.3 4.0 collective-permute-done.7
  83.4 4.8 %reshape.187 = bf16[1536,768]{1,0:T(8,128)(2,1)} reshape(bf16[768,1536]{1,0:T(8,128)(2,1)} %convolution_convert_fusion) | data formatting | bytes 4718592 | tf_op jit(solution)/shard_map/reshape | solution.py:189
  91.1 4.1 convolution_convert_fusion.1
  95.1 28.8 %concatenate.75 = bf16[3872,768]{1,0:T(8,128)(2,1)} concatenate(bf16[1536,768]{1,0:T(8,128)(2,1)} %convolution_convert_fusion.1, bf16[1536,768]{1,0:T(8,128)(2,1)} %reshape.187, bf16[768,768]{1,0:T(8,128)(2,1)} %convolution_convert_fusion.4, bf16[1,768]{1,0:T(2,128)(2,1)S(1)} %copy-done.36, bf16[1,768]{1,0:T(2,128)(2,1)S(1)} %reshape.189, bf16[1,768]{1,0:T(2,128)(2,1)S(1)} %reshape.190, ...), dimensions={0} | concatenate | bytes 11894784 | tf_op jit(solution)/shard_map/concatenate | solution.py:189
  123.9 3.6 constant_dynamic-slice_fusion.4
  133.0 14.3 %multiply_convert_fusion = bf16[3,1312,1312]{1,2,0:T(8,128)(2,1)} fusion(bf16[1312,3,64]{0,2,1:T(8,128)(2,1)S(1)} %bitcast.85, bf16[1312,3,64]{0,2,1:T(8,128)(2,1)S(1)} %bitcast.90, f32[3,1312]{1,0:T(4,128)S(1)} %bitcast.97, f32[3,1312]{1,0:T(4,128)S(1)} %broadcast_divide_fusion, f32[3,1312,1312]{1,2,0:T(8,128)} %get-tuple-element.119), kind=kOutput, calls=%fused_computation.2 | convolution fusion | flops 691980288 | bytes 32023296 | tf_op jit(solution)/shard_map/qhd,khd->hqk/dot_general | solution.py:196
  147.3 9.4 %fusion.11 = bf16[3,64,1312]{2,1,0:T(8,128)(2,1)} fusion(bf16[1312,3,64]{0,2,1:T(8,128)(2,1)S(1)} %bitcast.86, f32[3,1312]{1,0:T(4,128)S(1)} %broadcast_divide_fusion, bf16[1312,3,64]{0,2,1:T(8,128)(2,1)S(1)} %bitcast.82, bf16[1312,3,64]{0,2,1:T(8,128)(2,1)S(1)} %bitcast.78), kind=kOutput, calls=%fused_computation.37 | convolution fusion | flops 1348069504 | bytes 2030976 | tf_op jit(solution)/shard_map/hqk,qhd->khd/dot_general | solution.py:198
  156.7 6.1 %fusion.10 = bf16[3,64,1312]{2,1,0:T(8,128)(2,1)S(1)} fusion(bf16[1312,3,64]{0,2,1:T(8,128)(2,1)S(1)} %bitcast.79, bf16[3,1312,1312]{1,2,0:T(8,128)(2,1)} %multiply_convert_fusion), kind=kOutput, calls=%fused_computation.35 | convolution fusion | flops 661499904 | bytes 11335680 | tf_op jit(solution)/shard_map/hqk,khd->qhd/dot_general | solution.py:199
  167.4 4.6 %multiply_reduce_fusion = (bf16[768]{0:T(1024)(128)(2,1)S(1)}, f32[1312]{0:T(1024)S(1)}, f32[1312]{0:T(1024)S(1)}, bf16[768]{0:T(1024)(128)(2,1)S(1)}, f32[1312,768]{1,0:T(8,128)S(1)}) fusion(f32[1312,768]{1,0:T(8,128)S(1)} %copy-done.4, f32[1312]{0:T(1024)S(1)} %add_rsqrt_fusion, f32[1312]{0:T(1024)S(1)} %broadcast_multiply_fusion.2, ...), kind=kOutput, calls=%fused_computation.12 | convolution fusion | flops 1177026560 | bytes 10484224 | tf_op jit(solution)/shard_map/dot_general | solution.py:102
  189.7 7.1 %collective-permute-done.24 = bf16[968,768]{1,0:T(8,128)(2,1)} collective-permute-done((bf16[968,768]{1,0:T(8,128)(2,1)}, bf16[968,768]{1,0:T(8,128)(2,1)}, u32[]{:S(2)}, u32[]{:S(2)}) %collective-permute-start.24) | collective-permute-done | bytes 1486880 | tf_op jit(solution)/shard_map/ppermute | solution.py:25
  207.3 5.8 %collective-permute-done.25 = bf16[484,768]{1,0:T(8,128)(2,1)} collective-permute-done((bf16[484,768]{1,0:T(8,128)(2,1)}, bf16[484,768]{1,0:T(8,128)(2,1)}, u32[]{:S(2)}, u32[]{:S(2)}) %collective-permute-start.25) | collective-permute-done | bytes 743456 | tf_op jit(solution)/shard_map/ppermute | solution.py:25
  219.3 7.3 %collective-permute-done.26 = bf16[242,768]{1,0:T(8,128)(2,1)S(1)} collective-permute-done((bf16[242,768]{1,0:T(8,128)(2,1)S(1)}, bf16[242,768]{1,0:T(8,128)(2,1)S(1)}, u32[]{:S(2)}, u32[]{:S(2)}) %collective-permute-start.26) | collective-permute-done | bytes 371744 | tf_op jit(solution)/shard_map/ppermute | solution.py:25
  230.1 9.1 %collective-permute-done.27 = bf16[121,768]{1,0:T(8,128)(2,1)S(1)} collective-permute-done((bf16[121,768]{1,0:T(8,128)(2,1)S(1)}, bf16[121,768]{1,0:T(8,128)(2,1)S(1)}, u32[]{:S(2)}, u32[]{:S(2)}) %collective-permute-start.27) | collective-permute-done | bytes 185888 | tf_op jit(solution)/shard_map/ppermute | solution.py:25
  245.8 4.0 collective-permute-done.28
  254.9 7.5 %collective-permute-done.29 = bf16[242,768]{1,0:T(8,128)(2,1)} collective-permute-done((bf16[242,768]{1,0:T(8,128)(2,1)}, bf16[242,768]{1,0:T(8,128)(2,1)}, u32[]{:S(2)}, u32[]{:S(2)}) %collective-permute-start.29) | collective-permute-done | bytes 371744 | tf_op jit(solution)/shard_map/ppermute | solution.py:25
  271.6 5.0 %collective-permute-done.30 = bf16[484,768]{1,0:T(8,128)(2,1)} collective-permute-done((bf16[484,768]{1,0:T(8,128)(2,1)}, bf16[484,768]{1,0:T(8,128)(2,1)}, u32[]{:S(2)}, u32[]{:S(2)}) %collective-permute-start.30) | collective-permute-done | bytes 743456 | tf_op jit(solution)/shard_map/ppermute | solution.py:25
  291.2 9.1 %collective-permute-done.31 = bf16[968,768]{1,0:T(8,128)(2,1)} collective-permute-done((bf16[968,768]{1,0:T(8,128)(2,1)}, bf16[968,768]{1,0:T(8,128)(2,1)}, u32[]{:S(2)}, u32[]{:S(2)}) %collective-permute-start.31) | collective-permute-done | bytes 1486880 | tf_op jit(solution)/shard_map/ppermute | solution.py:25
  308.7 4.0 fusion.20
  312.7 32.5 %collective-permute-done.14 = bf16[328,768]{1,0:T(8,128)(2,1)} collective-permute-done((bf16[328,768]{1,0:T(8,128)(2,1)}, bf16[328,768]{1,0:T(8,128)(2,1)}, u32[]{:S(2)}, u32[]{:S(2)}) %collective-permute-start.14) | collective-permute-done | bytes 503840 | tf_op jit(solution)/shard_map/ppermute | solution.py:15
  350.5 4.2 maximum_convert_fusion.1
  354.7 9.0 %copy.92 = f32[3168,576]{1,0:T(8,128)} copy(f32[3168,576]{0,1:T(8,128)} %maximum_convert_fusion.1) | data formatting | bytes 14598144 | tf_op jit(solution)/shard_map/convert_element_type | solution.py:225
  363.7 6.8 %slice.159 = f32[4,768,576]{2,1,0:T(8,128)} slice(f32[4,792,576]{2,1,0:T(8,128)} %bitcast.72), slice={[0:4], [0:768], [0:576]} | slice | bytes 14155776 | tf_op jit(solution)/shard_map/slice | solution.py:229
  370.5 8.8 %copy.93 = f32[4,768,576]{1,2,0:T(8,128)} copy(f32[4,768,576]{2,1,0:T(8,128)} %slice.159) | data formatting | bytes 14155776 | tf_op jit(solution)/shard_map/slice | solution.py:229
  379.3 6.4 %copy.94 = f32[768,3,4,192]{0,3,2,1:T(8,128)} copy(f32[768,3,4,192]{0,3,1,2:T(8,128)} %bitcast.74) | data formatting | bytes 14155776 | tf_op jit(solution)/shard_map/transpose | solution.py:229
  385.7 8.1 %copy.95 = f32[768,2304]{1,0:T(8,128)} copy(f32[768,2304]{0,1:T(8,128)} %bitcast.75) | data formatting | bytes 14155776
  399.6 5.3 %maximum_convert_fusion = f32[3872,768]{1,0:T(8,128)} fusion(bf16[1936,768]{1,0:T(8,128)(2,1)S(1)} %get-tuple-element.77, bf16[1936,768]{1,0:T(8,128)(2,1)S(1)} %get-tuple-element.76), kind=kLoop, calls=%fused_computation.9 | loop fusion | flops 11894784 | bytes 17842176 | tf_op jit(solution)/shard_map/convert_element_type | solution.py:231
  408.1 8.0 %fusion.55 = (f32[1536,768]{1,0:T(8,128)}, f32[1536,768]{1,0:T(8,128)}) fusion(f32[3872,768]{1,0:T(8,128)} %maximum_convert_fusion), kind=kLoop, calls=%fused_computation.175 | loop fusion | bytes 18874368 | tf_op jit(solution)/shard_map/slice | solution.py:247
  416.7 6.2 %reshape.193 = f32[768,1536]{1,0:T(8,128)} reshape(f32[1536,768]{1,0:T(8,128)} %get-tuple-element.75) | data formatting | bytes 9437184 | tf_op jit(solution)/shard_map/reshape | solution.py:245
  (248 shorter events, 154.5 us)
Async XLA Ops:
  0.7 14.9 %collective-permute-start.1 = (bf16[328,768]{1,0:T(8,128)(2,1)}, bf16[328,768]{1,0:T(8,128)(2,1)}, u32[]{:S(2)}, u32[]{:S(2)}) collective-permute-start(bf16[328,768]{1,0:T(8,128)(2,1)} %bitcast.98), channel_id=1, source_target_pairs={{0,2},{1,3},{2,0},{3,1},{4,6},{5,7},{6,4},{7,5},{8,10},{9,11},{10,... | collective-permute-start | bytes 1511432 | tf_op jit(solution)/shard_map/ppermute | solution.py:15
  4.4 13.2 %collective-permute-start.4 = (s32[328]{0:T(512)S(1)}, s32[328]{0:T(512)S(1)}, u32[]{:S(2)}, u32[]{:S(2)}) collective-permute-start(s32[328]{0:T(512)S(1)} %reduce.4), channel_id=1, source_target_pairs={{0,2},{1,3},{2,0},{3,1},{4,6},{5,7},{6,4},{7,5},{8,10},{9,11},{10,... | collective-permute-start | bytes 3944 | tf_op jit(solution)/shard_map/ppermute | solution.py:15
  4.6 15.3 %collective-permute-start.3 = (s32[328]{0:T(512)S(1)}, s32[328]{0:T(512)S(1)}, u32[]{:S(2)}, u32[]{:S(2)}) collective-permute-start(s32[328]{0:T(512)S(1)} %reduce.4), channel_id=1, source_target_pairs={{0,1},{1,0},{2,3},{3,2},{4,5},{5,4},{6,7},{7,6},{8,9},{9,8},{10,11... | collective-permute-start | bytes 3944 | tf_op jit(solution)/shard_map/ppermute | solution.py:15
  4.6 17.5 %collective-permute-start = (bf16[328,768]{1,0:T(8,128)(2,1)}, bf16[328,768]{1,0:T(8,128)(2,1)}, u32[]{:S(2)}, u32[]{:S(2)}) collective-permute-start(bf16[328,768]{1,0:T(8,128)(2,1)} %bitcast.99), channel_id=1, source_target_pairs={{0,1},{1,0},{2,3},{3,2},{4,5},{5,4},{6,7},{7,6},{8,9},{9,8},{10,11... | collective-permute-start | bytes 1511432 | tf_op jit(solution)/shard_map/ppermute | solution.py:15
  15.5 6.6 %collective-permute-start.2 = (bf16[328,768]{1,0:T(8,128)(2,1)}, bf16[328,768]{1,0:T(8,128)(2,1)}, u32[]{:S(2)}, u32[]{:S(2)}) collective-permute-start(bf16[328,768]{1,0:T(8,128)(2,1)} %collective-permute-done.1), channel_id=1, source_target_pairs={{0,1},{1,0},{2,3},{3,2},{4,5},{5,4},{6,7},{7,6},{8,9},{9,8},{10,11... | collective-permute-start | bytes 1511432 | tf_op jit(solution)/shard_map/ppermute | solution.py:15
  56.8 6.5 %collective-permute-start.6 = (bf16[328,192]{1,0:T(8,128)(2,1)}, bf16[328,192]{1,0:T(8,128)(2,1)}, u32[]{:S(2)}, u32[]{:S(2)}) collective-permute-start(bf16[328,192]{1,0:T(8,128)(2,1)} %copy.73), channel_id=1, source_target_pairs={{0,3},{1,2},{2,1},{3,0},{4,7},{5,6},{6,5},{7,4},{8,11},{9,10},{10,... | collective-permute-start | bytes 377864 | tf_op jit(solution)/shard_map/ppermute | solution.py:15
  58.3 8.9 %collective-permute-start.7 = (bf16[328,192]{1,0:T(8,128)(2,1)}, bf16[328,192]{1,0:T(8,128)(2,1)}, u32[]{:S(2)}, u32[]{:S(2)}) collective-permute-start(bf16[328,192]{1,0:T(8,128)(2,1)} %copy.74), channel_id=1, source_target_pairs={{0,2},{1,3},{2,0},{3,1},{4,6},{5,7},{6,4},{7,5},{8,10},{9,11},{10,... | collective-permute-start | bytes 377864 | tf_op jit(solution)/shard_map/ppermute | solution.py:15
  58.7 8.6 %collective-permute-start.8 = (bf16[328,192]{1,0:T(8,128)(2,1)}, bf16[328,192]{1,0:T(8,128)(2,1)}, u32[]{:S(2)}, u32[]{:S(2)}) collective-permute-start(bf16[328,192]{1,0:T(8,128)(2,1)} %copy.75), channel_id=1, source_target_pairs={{0,1},{1,0},{2,3},{3,2},{4,5},{5,4},{6,7},{7,6},{8,9},{9,8},{10,11... | collective-permute-start | bytes 377864 | tf_op jit(solution)/shard_map/ppermute | solution.py:15
  89.2 40.0 %collective-permute-start.9 = (bf16[328,192]{1,0:T(8,128)(2,1)}, bf16[328,192]{1,0:T(8,128)(2,1)S(1)}, u32[]{:S(2)}, u32[]{:S(2)}) collective-permute-start(bf16[328,192]{1,0:T(8,128)(2,1)} %get-tuple-element.109), channel_id=1, source_target_pairs={{0,1},{1,0},{2,3},{3,2},{4,5},{5,4},{6,7},{7,6},{8,9},{9,8},{10,11... | collective-permute-start | bytes 377864 | tf_op jit(solution)/shard_map/ppermute | solution.py:15
  89.2 40.0 %collective-permute-start.10 = (bf16[328,192]{1,0:T(8,128)(2,1)}, bf16[328,192]{1,0:T(8,128)(2,1)S(1)}, u32[]{:S(2)}, u32[]{:S(2)}) collective-permute-start(bf16[328,192]{1,0:T(8,128)(2,1)} %get-tuple-element.110), channel_id=1, source_target_pairs={{0,2},{1,3},{2,0},{3,1},{4,6},{5,7},{6,4},{7,5},{8,10},{9,11},{10,... | collective-permute-start | bytes 377864 | tf_op jit(solution)/shard_map/ppermute | solution.py:15
  90.9 38.4 %collective-permute-start.11 = (bf16[328,192]{1,0:T(8,128)(2,1)}, bf16[328,192]{1,0:T(8,128)(2,1)S(1)}, u32[]{:S(2)}, u32[]{:S(2)}) collective-permute-start(bf16[328,192]{1,0:T(8,128)(2,1)} %get-tuple-element.111), channel_id=1, source_target_pairs={{0,3},{1,2},{2,1},{3,0},{4,7},{5,6},{6,5},{7,4},{8,11},{9,10},{10,... | collective-permute-start | bytes 377864 | tf_op jit(solution)/shard_map/ppermute | solution.py:15
  128.9 43.3 %collective-permute-start.23 = (bf16[1936,768]{1,0:T(8,128)(2,1)}, bf16[1936,768]{1,0:T(8,128)(2,1)}, u32[]{:S(2)}, u32[]{:S(2)}) collective-permute-start(bf16[1936,768]{1,0:T(8,128)(2,1)} %constant_dynamic-slice_fusion.4), channel_id=1, source_target_pairs={{0,1},{1,0},{2,3},{3,2},{4,5},{5,4},{6,7},{7,6},{8,9},{9,8},{10,11... | collective-permute-start | bytes 8921096 | tf_op jit(solution)/shard_map/ppermute | solution.py:25
  177.0 19.8 %collective-permute-start.24 = (bf16[968,768]{1,0:T(8,128)(2,1)}, bf16[968,768]{1,0:T(8,128)(2,1)}, u32[]{:S(2)}, u32[]{:S(2)}) collective-permute-start(bf16[968,768]{1,0:T(8,128)(2,1)} %constant_dynamic-slice_fusion.3), channel_id=1, source_target_pairs={{0,4},{1,9},{2,6},{3,11},{4,0},{5,13},{6,2},{7,15},{8,12},{9,1},{1... | collective-permute-start | bytes 4460552 | tf_op jit(solution)/shard_map/ppermute | solution.py:25
  189.3 13.5 %collective-permute-start.15 = (bf16[396,576]{1,0:T(8,128)(2,1)S(1)}, bf16[396,576]{1,0:T(8,128)(2,1)}, u32[]{:S(2)}, u32[]{:S(2)}) collective-permute-start(bf16[396,576]{1,0:T(8,128)(2,1)S(1)} %copy.84), channel_id=1, source_target_pairs={{0,4},{1,9},{2,6},{3,11},{4,0},{5,13},{6,2},{7,15},{8,12},{9,1},{1... | collective-permute-start | bytes 1368584 | tf_op jit(solution)/shard_map/ppermute | solution.py:25
  201.1 11.9 %collective-permute-start.25 = (bf16[484,768]{1,0:T(8,128)(2,1)}, bf16[484,768]{1,0:T(8,128)(2,1)}, u32[]{:S(2)}, u32[]{:S(2)}) collective-permute-start(bf16[484,768]{1,0:T(8,128)(2,1)} %constant_dynamic-slice_fusion.2), channel_id=1, source_target_pairs={{0,2},{1,5},{2,0},{3,7},{4,6},{5,1},{6,4},{7,3},{8,10},{9,13},{10,... | collective-permute-start | bytes 2230280 | tf_op jit(solution)/shard_map/ppermute | solution.py:25
  205.7 10.7 %collective-permute-start.16 = (bf16[198,576]{0,1:T(8,128)(2,1)}, bf16[198,576]{0,1:T(8,128)(2,1)S(1)}, u32[]{:S(2)}, u32[]{:S(2)}) collective-permute-start(bf16[198,576]{0,1:T(8,128)(2,1)} %constant_dynamic-slice_fusion.6), channel_id=1, source_target_pairs={{0,8},{1,5},{2,10},{3,7},{4,12},{5,1},{6,14},{7,3},{8,0},{9,13},{1... | collective-permute-start | bytes 684296 | tf_op jit(solution)/shard_map/ppermute | solution.py:25
  214.5 12.2 %collective-permute-start.26 = (bf16[242,768]{1,0:T(8,128)(2,1)S(1)}, bf16[242,768]{1,0:T(8,128)(2,1)S(1)}, u32[]{:S(2)}, u32[]{:S(2)}) collective-permute-start(bf16[242,768]{1,0:T(8,128)(2,1)S(1)} %constant_dynamic-slice_fusion.1), channel_id=1, source_target_pairs={{0,8},{1,3},{2,10},{3,1},{4,12},{5,7},{6,14},{7,5},{8,0},{9,11},{1... | collective-permute-start | bytes 1115144 | tf_op jit(solution)/shard_map/ppermute | solution.py:25
  216.7 11.0 %collective-permute-start.17 = (bf16[99,576]{0,1:T(8,128)(2,1)S(1)}, bf16[99,576]{0,1:T(8,128)(2,1)S(1)}, u32[]{:S(2)}, u32[]{:S(2)}) collective-permute-start(bf16[99,576]{0,1:T(8,128)(2,1)S(1)} %constant_dynamic-slice_fusion.5), channel_id=1, source_target_pairs={{0,16},{1,17},{2,18},{3,19},{4,20},{5,21},{6,22},{7,23},{8,24},{9,... | collective-permute-start | bytes 342152 | tf_op jit(solution)/shard_map/ppermute | solution.py:25
  226.9 12.3 %collective-permute-start.27 = (bf16[121,768]{1,0:T(8,128)(2,1)S(1)}, bf16[121,768]{1,0:T(8,128)(2,1)S(1)}, u32[]{:S(2)}, u32[]{:S(2)}) collective-permute-start(bf16[121,768]{1,0:T(8,128)(2,1)S(1)} %constant_dynamic-slice_fusion), channel_id=1, source_target_pairs={{0,16},{1,17},{2,18},{3,19},{4,20},{5,21},{6,22},{7,23},{8,24},{9,... | collective-permute-start | bytes 557576 | tf_op jit(solution)/shard_map/ppermute | solution.py:25
  227.8 14.5 %collective-permute-start.18 = (bf16[99,576]{0,1:T(8,128)(2,1)S(1)}, bf16[99,576]{0,1:T(8,128)(2,1)S(1)}, u32[]{:S(2)}, u32[]{:S(2)}) collective-permute-start(bf16[99,576]{0,1:T(8,128)(2,1)S(1)} %add_convert_fusion.9), channel_id=1, source_target_pairs={{0,16},{1,17},{2,18},{3,19},{4,20},{5,21},{6,22},{7,23},{8,24},{9,... | collective-permute-start | bytes 342152 | tf_op jit(solution)/shard_map/ppermute | solution.py:25
  239.3 10.5 %collective-permute-start.28 = (bf16[121,768]{1,0:T(8,128)(2,1)S(1)}, bf16[121,768]{1,0:T(8,128)(2,1)S(1)}, u32[]{:S(2)}, u32[]{:S(2)}) collective-permute-start(bf16[121,768]{1,0:T(8,128)(2,1)S(1)} %add_convert_fusion.8), channel_id=1, source_target_pairs={{0,16},{1,17},{2,18},{3,19},{4,20},{5,21},{6,22},{7,23},{8,24},{9,... | collective-permute-start | bytes 557576 | tf_op jit(solution)/shard_map/ppermute | solution.py:25
  242.5 10.0 %collective-permute-start.19 = (bf16[198,576]{0,1:T(8,128)(2,1)S(1)}, bf16[198,576]{0,1:T(8,128)(2,1)S(1)}, u32[]{:S(2)}, u32[]{:S(2)}) collective-permute-start(bf16[198,576]{0,1:T(8,128)(2,1)S(1)} %pad_maximum_fusion.15), channel_id=1, source_target_pairs={{0,8},{1,5},{2,10},{3,7},{4,12},{5,1},{6,14},{7,3},{8,0},{9,13},{1... | collective-permute-start | bytes 684296 | tf_op jit(solution)/shard_map/ppermute | solution.py:25
  250.7 11.8 %collective-permute-start.29 = (bf16[242,768]{1,0:T(8,128)(2,1)}, bf16[242,768]{1,0:T(8,128)(2,1)}, u32[]{:S(2)}, u32[]{:S(2)}) collective-permute-start(bf16[242,768]{1,0:T(8,128)(2,1)} %pad_maximum_fusion.12), channel_id=1, source_target_pairs={{0,8},{1,3},{2,10},{3,1},{4,12},{5,7},{6,14},{7,5},{8,0},{9,11},{1... | collective-permute-start | bytes 1115144 | tf_op jit(solution)/shard_map/ppermute | solution.py:25
  253.3 14.7 %collective-permute-start.20 = (bf16[396,576]{1,0:T(8,128)(2,1)S(1)}, bf16[396,576]{1,0:T(8,128)(2,1)}, u32[]{:S(2)}, u32[]{:S(2)}) collective-permute-start(bf16[396,576]{1,0:T(8,128)(2,1)S(1)} %copy.86), channel_id=1, source_target_pairs={{0,4},{1,9},{2,6},{3,11},{4,0},{5,13},{6,2},{7,15},{8,12},{9,1},{1... | collective-permute-start | bytes 1368584 | tf_op jit(solution)/shard_map/ppermute | solution.py:25
  264.7 11.9 %collective-permute-start.30 = (bf16[484,768]{1,0:T(8,128)(2,1)}, bf16[484,768]{1,0:T(8,128)(2,1)}, u32[]{:S(2)}, u32[]{:S(2)}) collective-permute-start(bf16[484,768]{1,0:T(8,128)(2,1)} %pad_maximum_fusion.6), channel_id=1, source_target_pairs={{0,2},{1,5},{2,0},{3,7},{4,6},{5,1},{6,4},{7,3},{8,10},{9,13},{10,... | collective-permute-start | bytes 2230280 | tf_op jit(solution)/shard_map/ppermute | solution.py:25
  271.5 12.6 %collective-permute-start.21 = (bf16[792,576]{1,0:T(8,128)(2,1)}, bf16[792,576]{1,0:T(8,128)(2,1)S(1)}, u32[]{:S(2)}, u32[]{:S(2)}) collective-permute-start(bf16[792,576]{1,0:T(8,128)(2,1)} %copy.89), channel_id=1, source_target_pairs={{0,1},{1,0},{2,3},{3,2},{4,5},{5,4},{6,7},{7,6},{8,9},{9,8},{10,11... | collective-permute-start | bytes 2737160 | tf_op jit(solution)/shard_map/ppermute | solution.py:25
  280.4 19.8 %collective-permute-start.31 = (bf16[968,768]{1,0:T(8,128)(2,1)}, bf16[968,768]{1,0:T(8,128)(2,1)}, u32[]{:S(2)}, u32[]{:S(2)}) collective-permute-start(bf16[968,768]{1,0:T(8,128)(2,1)} %pad_maximum_fusion.3), channel_id=1, source_target_pairs={{0,4},{1,9},{2,6},{3,11},{4,0},{5,13},{6,2},{7,15},{8,12},{9,1},{1... | collective-permute-start | bytes 4460552 | tf_op jit(solution)/shard_map/ppermute | solution.py:25
  284.1 21.1 %collective-permute-start.13 = (bf16[328,768]{1,0:T(8,128)(2,1)}, bf16[328,768]{1,0:T(8,128)(2,1)}, u32[]{:S(2)}, u32[]{:S(2)}) collective-permute-start(bf16[328,768]{1,0:T(8,128)(2,1)} %get-tuple-element.88), channel_id=1, source_target_pairs={{0,1},{1,0},{2,3},{3,2},{4,5},{5,4},{6,7},{7,6},{8,9},{9,8},{10,11... | collective-permute-start | bytes 1511432 | tf_op jit(solution)/shard_map/ppermute | solution.py:15
  289.9 57.8 %collective-permute-start.22 = (bf16[1584,576]{0,1:T(8,128)(2,1)}, bf16[1584,576]{0,1:T(8,128)(2,1)}, u32[]{:S(2)}, u32[]{:S(2)}) collective-permute-start(bf16[1584,576]{0,1:T(8,128)(2,1)} %pad_maximum_fusion.1), channel_id=1, source_target_pairs={{0,2},{1,3},{2,0},{3,1},{4,6},{5,7},{6,4},{7,5},{8,10},{9,11},{10,... | collective-permute-start | bytes 5474312 | tf_op jit(solution)/shard_map/ppermute | solution.py:25
  304.7 91.4 %collective-permute-start.32 = (bf16[1936,768]{1,0:T(8,128)(2,1)}, bf16[1936,768]{1,0:T(8,128)(2,1)}, u32[]{:S(2)}, u32[]{:S(2)}) collective-permute-start(bf16[1936,768]{1,0:T(8,128)(2,1)} %pad_maximum_fusion), channel_id=1, source_target_pairs={{0,1},{1,0},{2,3},{3,2},{4,5},{5,4},{6,7},{7,6},{8,9},{9,8},{10,11... | collective-permute-start | bytes 8921096 | tf_op jit(solution)/shard_map/ppermute | solution.py:25
  304.7 8.0 %collective-permute-start.12 = (bf16[328,768]{1,0:T(8,128)(2,1)}, bf16[328,768]{1,0:T(8,128)(2,1)}, u32[]{:S(2)}, u32[]{:S(2)}) collective-permute-start(bf16[328,768]{1,0:T(8,128)(2,1)} %get-tuple-element.87), channel_id=1, source_target_pairs={{0,1},{1,0},{2,3},{3,2},{4,5},{5,4},{6,7},{7,6},{8,9},{9,8},{10,11... | collective-permute-start | bytes 1511432 | tf_op jit(solution)/shard_map/ppermute | solution.py:15
  307.4 37.7 %collective-permute-start.14 = (bf16[328,768]{1,0:T(8,128)(2,1)}, bf16[328,768]{1,0:T(8,128)(2,1)}, u32[]{:S(2)}, u32[]{:S(2)}) collective-permute-start(bf16[328,768]{1,0:T(8,128)(2,1)} %fusion.22), channel_id=1, source_target_pairs={{0,2},{1,3},{2,0},{3,1},{4,6},{5,7},{6,4},{7,5},{8,10},{9,11},{10,... | collective-permute-start | bytes 1511432 | tf_op jit(solution)/shard_map/ppermute | solution.py:15
  (46 other events, 290.1 us)

commit v2 on v1

v2 whole, which is shorter than its diff:
```python
import functools

import jax
import jax.numpy as jnp
from jax import lax
from jax.experimental import pallas as pl
from jax.experimental.pallas import tpu as pltpu
from jax.sharding import PartitionSpec as P

HEADS = 12
HEAD = 64
BF = jnp.bfloat16
F32 = jnp.float32
BOTH = ("scene", "view")
MINE = HEADS // 4 * HEAD
PAD = 256
MIB = 1 << 20


def swap(value, axis, mask):
    count = lax.axis_size(axis)
    return lax.ppermute(value, axis, [(i, i ^ mask) for i in range(count)])


def swap_by_core(value, masks):
    scenes, views = lax.axis_size("scene"), lax.axis_size("view")
    pairs = []
    for s in range(scenes):
        for v in range(views):
            ds, dv = masks[v % 2]
            pairs.append((s * views + v, (s ^ ds) * views + (v ^ dv)))
    return lax.ppermute(value, BOTH, pairs)


def side_of(masks, core):
    scene, view = lax.axis_index("scene"), lax.axis_index("view")
    bits = [((scene & ds) + (view & dv) > 0).astype(jnp.int32) for ds, dv in masks]
    return jnp.where(core == 0, bits[0], bits[1])


def code_of(stages, core):
    total = 0
    for masks in stages:
        total = 2 * total + side_of(masks, core)
    return total


X, Y, Z1, Z2 = (1, 0), (0, 2), (2, 0), (4, 0)
WIDE = ((X, Z1), (Y, X), (Z1, Y), (Z2, Z2))
THIN = ((Y, Y), (Z1, Z1), (X, X), (Z2, Z2))
SCENE = ((X, Z1), (Z1, X), (Z2, Z2))


def rounded(value):
    return lax.optimization_barrier(lax.reduce_precision(value, 8, 7).astype(BF))


def whole_slice(value):
    bit = 8
    while bit < lax.axis_size("scene"):
        value = rounded(value.astype(F32) + swap(value, "scene", bit).astype(F32))
        bit *= 2
    return value


def by_view(blocks, me):
    a, b, c, d = blocks
    one = (me & 1) == 1
    a, b = jnp.where(one, b, a), jnp.where(one, a, b)
    c, d = jnp.where(one, d, c), jnp.where(one, c, d)
    two = (me & 2) == 2
    a, c = jnp.where(two, c, a), jnp.where(two, a, c)
    b, d = jnp.where(two, d, b), jnp.where(two, b, d)
    return a, b, c, d


def normalise(values):
    centre = values - jnp.mean(values, axis=-1, keepdims=True)
    rstd = lax.rsqrt(jnp.mean(centre * centre, axis=-1, keepdims=True) + 1e-05)
    return centre * rstd, rstd


def norm_back(grad, unit, rstd):
    return (
        grad
        - jnp.mean(grad, axis=-1, keepdims=True)
        - unit * jnp.mean(grad * unit, axis=-1, keepdims=True)
    ) * rstd


def dot(a, b):
    return jnp.dot(a, b, preferred_element_type=F32)


def tdot(a, b):
    return lax.dot_general(a, b, (((0,), (0,)), ((), ())), preferred_element_type=F32)


def dott(a, b):
    return lax.dot_general(a, b, (((1,), (1,)), ((), ())), preferred_element_type=F32)


def split3(values):
    high = values.astype(BF)
    rest = values - high.astype(F32)
    middle = rest.astype(BF)
    return high, middle, (rest - middle.astype(F32)).astype(BF)


def onehot_t(cameras, groups):
    rows = lax.broadcasted_iota(jnp.int32, (groups, cameras.shape[1]), 0)
    return (rows == cameras).astype(F32).astype(BF)


class Incoming:
    def __init__(self, source, buffer, sem):
        self.copy, self.buffer, self.there = pltpu.make_async_copy(source, buffer, sem), buffer, False
        self.copy.start()

    def __call__(self):
        if not self.there:
            self.copy.wait()
            self.there = True
        return self.buffer


class Present:
    def __init__(self, ref):
        self.buffer = ref

    def __call__(self):
        return self.buffer


class Outgoing:
    def __init__(self, target, buffer, sems, moves):
        self.target, self.ref, self.sems, self.moves = target, buffer, sems, moves

    def send(self, here=None, there=None):
        source = self.ref if here is None else self.ref.at[here]
        target = self.target if there is None else self.target.at[there]
        move = pltpu.make_async_copy(source, target, self.sems.at[len(self.moves)])
        move.start()
        self.moves.append(move)


class Operand:
    def __init__(self, array, *, home=False, ready=False, cut=None, shape=None, room=None):
        self.array, self.ready, self.cut, self.room, self.apart = array, ready, cut, room, False
        if home:
            self.array = pltpu.with_memory_space_constraint(array, pltpu.HBM)
        self.shape = array.shape if shape is None else shape


def apart(array):
    operand = Operand(array, home=True)
    operand.apart = True
    return operand


def home(array, **more):
    return Operand(array, home=True, **more)


def ready(array):
    return Operand(array, ready=True)


def staged(body, args, outs, *, name, mib, scratch=(), code=None, held=(), buffers=None):
    buffers = buffers or {}
    args = [a if isinstance(a, Operand) else Operand(a) for a in args]
    n_code, n_in, n_held, n_out = int(code is not None), len(args), len(held), len(outs)
    loads = [i for i, a in enumerate(args) if not (a.ready or a.apart)]

    def kernel(*refs):
        code_ref = refs[0] if n_code else None
        refs = refs[n_code:]
        ins, refs = refs[:n_in], refs[n_in + n_held :]
        targets, refs = refs[:n_out], refs[n_out:]
        in_bufs, refs = refs[: len(loads)], refs[len(loads) :]
        out_bufs, refs = refs[:n_out], refs[n_out:]
        in_sems, out_sems, rest = refs[0], refs[1], refs[2:]
        arrivals = [Present(ref) for ref in ins]
        for n, i in enumerate(loads):
            source = ins[i] if args[i].cut is None else ins[i].at[args[i].cut]
            buffer = in_bufs[n] if args[i].room is None else in_bufs[n].at[: args[i].shape[0]]
            arrivals[i] = Incoming(source, buffer, in_sems.at[n])
            if args[i].room is not None:
                arrivals[i].buffer = in_bufs[n]
        moves = []
        leaving = [Outgoing(t, b, out_sems, moves) for t, b in zip(targets, out_bufs, strict=True)]
        body(code_ref, arrivals, leaving, *rest)
        for arrival in arrivals:
            arrival()
        for move in moves:
            move.wait()

    anywhere, vmem = pl.BlockSpec(memory_space=pl.ANY), pl.BlockSpec(memory_space=pltpu.VMEM)
    specs = [pl.BlockSpec(memory_space=pltpu.SMEM)] * n_code
    specs += [vmem if a.ready else anywhere for a in args] + [anywhere] * n_held
    operands = ([code] if n_code else []) + [a.array for a in args]
    operands += [pltpu.with_memory_space_constraint(a, pltpu.HBM) for a in held]
    bufs = []
    for i in loads:
        shape = args[i].shape
        if args[i].room is not None:
            shape = (args[i].room, *shape[1:])
        bufs.append(pltpu.VMEM(shape, args[i].array.dtype))
    return pl.pallas_call(
        kernel,
        in_specs=specs,
        out_specs=[anywhere] * n_out,
        out_shape=[pltpu.HBM(shape, dtype) for shape, dtype in outs],
        scratch_shapes=bufs
        + [pltpu.VMEM(buffers.get(i, o[0]), o[1]) for i, o in enumerate(outs)]
        + [pltpu.SemaphoreType.DMA((max(len(loads), 1),)), pltpu.SemaphoreType.DMA((48,))]
        + list(scratch),
        input_output_aliases={n_code + n_in + i: i for i in range(n_held)},
        compiler_params=pltpu.CompilerParams(vmem_limit_bytes=mib * MIB),
        cost_estimate=pl.CostEstimate(flops=0, bytes_accessed=0, transcendentals=0),
        name=name,
    )(*operands)


def project_rows(tokens, cams, embedding, gain, shift, weight, outs, there, hold_ref, summed=None):
    normed, unit, rstd, *triple = outs
    rows = tokens[0].buffer.shape[0]
    pair = 2 * rows
    table = jnp.concatenate(split3(embedding()[...]), 0)
    for at, (x, c) in enumerate(zip(tokens, cams, strict=True)):
        hot = onehot_t(c()[...], embedding().shape[0])
        values = x()[...].astype(F32) + tdot(jnp.concatenate([hot] * 3, 0), table)
        if at == 0 and summed is not None:
            summed.ref[...] = values
            summed.send()
        values, scale = normalise(values)
        hold_ref[pl.ds(at * rows, rows), :] = values
        rstd.ref[pl.ds(at * rows, rows), :] = scale
    values = hold_ref[...]
    low = (values * gain()[...] + shift()[...]).astype(BF)
    normed.ref[...] = low
    lane = lax.broadcasted_iota(jnp.int32, (pair, PAD), 1)
    for i, (ref, first, out) in enumerate(triple):
        block = dot(low, weight()[:, i * PAD : (i + 1) * PAD])
        if i == 0:
            block = block * HEAD**-0.5
        if i == 2:
            block = jnp.where(lane < MINE, block, 1.0)
        ref[first : first + pair, :] = block.astype(BF)
        out.send((pl.ds(first, pair),), there)
    normed.send(None, there)
    unit.ref[...] = values.astype(BF)
    unit.send(None, there)
    rstd.send(None, there)


def project_outs(total, width):
    outs = [((total, width), BF), ((total, width), BF), ((total, 1), F32)]
    return outs + [((total, PAD), BF)] * 3


def project_body(_, ins, outs, hold_ref):
    xa, xb, ca, cb, embedding, gain, shift, weight = ins
    there = (pl.ds(0, hold_ref.shape[0]),)
    triple = [(out.ref, 0, out) for out in outs[3:6]]
    project_rows((xa, xb), (ca, cb), embedding, gain, shift, weight, [*outs[:3], *triple], there, hold_ref, outs[6])


def project(xa, xb, ca, cb, embedding, gain, shift, weight):
    rows, width = xa.shape[-2:]
    pair, total = 2 * rows, 4 * rows
    outs = project_outs(total, width)
    return staged(
        project_body,
        [xa, xb, ca, cb, embedding, gain, shift, weight],
        [*outs, ((rows, width), F32)],
        name="project",
        mib=32,
        scratch=[pltpu.VMEM((pair, width), F32)],
        buffers={i: (pair, o[0][1]) for i, o in enumerate(outs)},
    )


def blocks_of(total):
    return [(at, min(256, total - at)) for at in range(0, total, 256)]


def one_head(block, head):
    lane = lax.broadcasted_iota(jnp.int32, block.shape, 1) // HEAD
    return jnp.where(lane == head, block, jnp.zeros_like(block))


def attend_rows(q_ref, keys, values_of, outs, vt_ref, mt_ref, it_ref):
    e, first, second, mix, inv = outs
    pair, heads = q_ref.shape[0], e.ref.shape[0]
    work = [(h, at, size) for h in range(heads) for at, size in blocks_of(pair)]

    def scores(h, at, size):
        return dott(keys()[...], one_head(q_ref[at : at + size, :], h))

    ahead = scores(*work[0])
    vt_ref[...] = values_of()[...].astype(F32).T.astype(BF)
    mt_ref[...] = jnp.zeros_like(mt_ref)
    it_ref[...] = jnp.zeros_like(it_ref)
    for i, (h, at, size) in enumerate(work):
        here = ahead
        if i + 1 < len(work):
            ahead = scores(*work[i + 1])
        mine = slice(h * HEAD, (h + 1) * HEAD)
        expo = jnp.exp(here - jnp.max(here, 0, keepdims=True)).astype(BF)
        cut = (h, slice(None), slice(at, at + size))
        e.ref[cut] = expo
        e.send((h, slice(None), pl.ds(at, size)), (h, slice(None), pl.ds(at, size)))
        values = jnp.concatenate([vt_ref[mine, :], vt_ref[MINE : MINE + 16, :]], 0)
        out = dot(values, expo)
        inverse = 1.0 / out[HEAD : HEAD + 1, :]
        mt_ref[mine, at : at + size] = out[:HEAD, :] * inverse
        it_ref[mine, at : at + size] = jnp.broadcast_to(inverse, (HEAD, size))
    mixed = mt_ref[...].T[:pair]
    first.ref[...] = mixed[: pair // 2, :MINE].astype(BF)
    first.send()
    second.ref[...] = mixed[pair // 2 :, :MINE].astype(BF)
    second.send()
    mix.ref[...] = mixed[:, :MINE]
    mix.send()
    inv.ref[...] = it_ref[...].T[:pair, :MINE]
    inv.send()


def attend_outs(total):
    pair, heads = total // 2, MINE // HEAD
    part, soft = ((pair // 2, MINE), BF), ((pair, MINE), F32)
    return [((heads, total, pair), BF), part, part, soft, soft]


def attend_scratch(total):
    wide = -(-(total // 2) // 128) * 128
    return [pltpu.VMEM((PAD, total), BF), pltpu.VMEM((PAD, wide), F32), pltpu.VMEM((PAD, wide), F32)]


def attend_body(_, ins, outs, *scratch):
    q, k, v = ins
    attend_rows(q(), k, v, outs, *scratch)


def attend(q, k, v):
    total = k.shape[0]
    pair = total // 2
    return staged(
        attend_body,
        [home(q, cut=(pl.ds(0, pair),), shape=(pair, PAD)), home(k), home(v)],
        attend_outs(total),
        name="attend",
        mib=32,
        scratch=attend_scratch(total),
    )


def second_body(_, ins, outs, hold_ref, *scratch):
    xa, xb, ca, cb, embedding, gain, shift, weight, k, v = ins
    pair = hold_ref.shape[0]
    there = (pl.ds(pair, pair),)
    triple = [(outs[3].ref, 0, outs[3]), (k.buffer, pair, outs[4]), (v.buffer, pair, outs[5])]
    outs[4].ref, outs[5].ref = k.buffer, v.buffer
    project_rows((xa, xb), (ca, cb), embedding, gain, shift, weight, [*outs[:3], *triple], there, hold_ref)
    attend_rows(outs[3].ref, k, v, outs[6:], *scratch)


def second_half(xa, xb, ca, cb, embedding, gain, shift, weight, held):
    rows, width = xa.shape[-2:]
    pair, total = 2 * rows, 4 * rows
    outs = project_outs(total, width)
    buffers = {i: (pair, o[0][1]) for i, o in enumerate(outs)}
    buffers[4] = buffers[5] = (16, PAD)
    first = dict(cut=(pl.ds(0, pair),), shape=(pair, PAD), room=total)
    return staged(
        second_body,
        [xa, xb, ca, cb, embedding, gain, shift, weight, home(held[4], **first), home(held[5], **first)],
        [*outs, *attend_outs(total)],
        name="second_half",
        mib=44,
        scratch=[pltpu.VMEM((pair, width), F32), *attend_scratch(total)],
        held=held,
        buffers=buffers,
    )


def back_body(code, ins, outs, g_ref, kt_ref, delta_ref, dq_ref, dka_ref, dva_ref, hold_ref, piece_ref):
    q, k, v, *ins = ins
    grads, mixes, invs, expos, normed = ins[:4], ins[4:6], ins[6:8], ins[8:-1], ins[-1]
    dqk, dv = outs[:2]
    total = q.buffer.shape[0]
    pair, rows = total // 2, grads[0].buffer.shape[0]
    heads = len(expos) // 2
    hold_ref[...] = jnp.zeros_like(hold_ref)
    for i, grad in enumerate(grads):
        hold_ref[i * rows : (i + 1) * rows, :MINE] = grad()[...].astype(F32)
    lane = lax.broadcasted_iota(jnp.int32, (8, PAD), 1) // HEAD
    pick = (lane == lax.broadcasted_iota(jnp.int32, (8, PAD), 0)).astype(F32).astype(BF)
    for i in range(2):
        here = slice(i * pair, (i + 1) * pair)
        hold_ref[here, :MINE] = hold_ref[here, :MINE] * invs[i]()[...]
        scaled = hold_ref[here, :].astype(BF)
        g_ref[here, :] = scaled
        hold_ref[here, :MINE] = scaled[:, :MINE].astype(F32) * mixes[i]()[...]
        prod = hold_ref[here, :]
        high = prod.astype(BF)
        low = (prod - high.astype(F32)).astype(BF)
        delta_ref[i, :, :pair] = dott(pick, high) + dott(pick, low)
    kt_ref[...] = k()[...].astype(F32).T.astype(BF)
    dq_ref[...] = jnp.zeros_like(dq_ref)
    work = [(h, i, at, size) for h in range(heads) for i in range(2) for at, size in blocks_of(pair)]

    def cut(ref, h, i, at, size):
        return one_head(ref[i * pair + at : i * pair + at + size, :], h)

    ahead_grad = cut(g_ref, *work[0])
    ahead = dott(v()[...], ahead_grad)
    for n, (h, i, at, size) in enumerate(work):
        grad, prob_grad = ahead_grad, ahead
        if n + 1 < len(work):
            ahead_grad = cut(g_ref, *work[n + 1])
            ahead = dott(v()[...], ahead_grad)
        expo = expos[2 * h + i]()[:, at : at + size]
        delta = delta_ref[i, h : h + 1, at : at + size]
        score_grad = (expo.astype(F32) * (prob_grad - delta)).astype(BF)
        value_part = dot(expo, grad)
        key_part = dot(score_grad, cut(q(), h, i, at, size))
        if n:
            value_part += dva_ref[...]
            key_part += dka_ref[...]
        dva_ref[...] = value_part
        dka_ref[...] = key_part
        mine = slice(h * HEAD, (h + 1) * HEAD)
        dq_ref[i, mine, at : at + size] = dot(kt_ref[mine, :], score_grad)
    for i in range(2):
        dq = dq_ref[i].T[:pair] * HEAD**-0.5
        dqk.ref[i * pair : (i + 1) * pair, :MINE] = dq[:, :MINE].astype(BF)
    dqk.ref[:, MINE:] = dka_ref[:, :MINE].astype(BF)
    dqk.send()
    dv.ref[...] = dva_ref[:, :MINE].astype(BF)
    dv.send()
    weight_grad(code, normed, dqk.ref, dv.ref, outs[2], outs[3], piece_ref)


PIECES = 8


def weight_grad(code, normed, dqk_ref, dv_ref, keep, send, hold_ref):
    width = normed().shape[1]
    rows = width // PIECES
    piece = rows + rows // 2
    mine = code[0]
    qk = tdot(normed()[...], dqk_ref[...]).astype(BF)
    v = tdot(normed()[...], dv_ref[...]).astype(BF)
    for p in range(PIECES):
        at = pl.multiple_of((p ^ mine) * piece, 16)
        hold_ref[pl.ds(at, rows), :] = qk[p * rows : (p + 1) * rows]
        at = pl.multiple_of((p ^ mine) * piece + rows, 16)
        top = v[p * rows : p * rows + rows // 2]
        low = v[p * rows + rows // 2 : (p + 1) * rows]
        hold_ref[pl.ds(at, rows // 2), :] = jnp.concatenate([top, low], 1)
    half = PIECES * piece // 2
    send.ref[...] = hold_ref[half:, :]
    send.send()
    keep.ref[...] = hold_ref[:half, :]
    keep.send()


def attend_back(codes, q, k, v, e0, e1, grads, mix0, mix1, inv0, inv1, normed):
    total, heads = k.shape[0], MINE // HEAD
    pair = total // 2
    wide = -(-pair // 128) * 128
    width = normed.shape[1]
    piece = width // PIECES * 3 // 2
    args = [home(q), home(k), home(v), *grads, home(mix0), home(mix1), home(inv0), home(inv1)]
    for h in range(heads):
        args += [home(e, cut=(h,), shape=(total, pair)) for e in (e0, e1)]
    args.append(home(normed))
    half = ((PIECES * piece // 2, 2 * MINE), BF)
    return staged(
        back_body,
        args,
        [((total, 2 * MINE), BF), ((total, MINE), BF), half, half],
        name="attend_back",
        mib=52,
        scratch=[
            pltpu.VMEM((total, PAD), BF),
            pltpu.VMEM((PAD, total), BF),
            pltpu.VMEM((2, 8, wide), F32),
            pltpu.VMEM((2, PAD, wide), F32),
            pltpu.VMEM((total, PAD), F32),
            pltpu.VMEM((total, PAD), F32),
            pltpu.VMEM((total, PAD), F32),
            pltpu.VMEM((PIECES * piece, 2 * MINE), BF),
        ],
        code=codes,
    )


STEP = 512


def feed_forward_body(code, ins, outs):
    summed, own, near, far, rest, combiner, baseline, gain, shift, expander, priming, squeezer, tangent = ins
    residual, own_wide, wide, own_slim, slim = outs
    me = code[2]
    first = code[3] == 0
    total = summed()[...] + baseline()[...]
    for r, block in ((2, far), (3, rest), (0, own), (1, near)):
        at = pl.multiple_of((me ^ r) * MINE, 16)
        total += dot(block()[...], combiner()[pl.ds(at, MINE), :])
    residual.ref[...] = total
    residual.send()
    unit, _ = normalise(total)
    low = (unit * gain()[...] + shift()[...]).astype(BF)
    own_slim.ref[...] = jnp.where(first, tangent()[...], low)
    own_slim.send()
    slim.ref[...] = jnp.where(first, low, tangent()[...])
    slim.send()
    for at in range(0, expander().shape[1], STEP):
        cut = slice(at, at + STEP)
        hidden = dot(low, expander()[:, cut]) + priming()[cut]
        back = dott(tangent()[...], squeezer()[cut, :])
        phi = 0.5 * (1.0 + lax.erf(hidden * (2.0**-0.5)))
        density = jnp.exp(-0.5 * hidden * hidden) * 0.3989422804014327
        active = (hidden * phi).astype(BF)
        grad = (back * (phi + hidden * density)).astype(BF)
        own_wide.ref[:, cut] = jnp.where(first, active, grad)
        wide.ref[:, cut] = jnp.where(first, grad, active)
        part = (slice(None), pl.ds(at, STEP))
        own_wide.send(part, part)
        wide.send(part, part)


def feed_forward(codes, summed, own, near, far, rest, combiner, baseline, gain, shift, expander, priming, squeezer, tangent):
    rows, width = summed.shape
    hid = expander.shape[1]
    weights = [ready(combiner), baseline, gain, shift, ready(expander), priming, ready(squeezer), ready(tangent)]
    return staged(
        feed_forward_body,
        [home(summed), own, near, far, rest, *weights],
        [((rows, width), F32), ((rows, hid), BF), ((rows, hid), BF), ((rows, width), BF), ((rows, width), BF)],
        name="feed_forward",
        mib=24,
        code=codes,
    )


def feed_back_body(code, ins, outs, grad_ref, sem):
    residual, tangent, expander, gain, combiner, own_wide, wide = ins
    residual_grad, low, *grads, rows = outs
    me = code[2]

    for core, source in enumerate((wide, own_wide)):

        @pl.when(code[3] == core)
        def _():
            pltpu.make_async_copy(source(), grad_ref, sem.at[0]).start()

    pltpu.make_async_copy(wide(), grad_ref, sem.at[0]).wait()
    second_grad = dott(grad_ref[...], expander()[...])
    unit, rstd = normalise(residual()[...])
    slope = tangent()[...].astype(F32)
    total = slope + norm_back(second_grad * gain()[...], unit, rstd)
    low.ref[...] = total.astype(BF)
    low.send()
    for r in (2, 3, 1, 0):
        at = pl.multiple_of((me ^ r) * MINE, 16)
        grads[r].ref[...] = dott(low.ref[...], combiner()[pl.ds(at, MINE), :]).astype(BF)
        grads[r].send()
    residual_grad.ref[...] = total
    residual_grad.send()
    width = total.shape[1]
    rows.ref[0:1, :] = jnp.sum(slope, 0, keepdims=True)
    rows.ref[1:2, :] = jnp.sum(low.ref[...].astype(F32), 0, keepdims=True)
    rows.ref[2:3, :] = jnp.sum(second_grad * unit, 0, keepdims=True)
    rows.ref[3:4, :] = jnp.sum(second_grad, 0, keepdims=True)
    for j in range(grad_ref.shape[1] // width):
        block = grad_ref[:, j * width : (j + 1) * width].astype(F32)
        rows.ref[4 + j : 5 + j, :] = jnp.sum(block, 0, keepdims=True)
    rows.ref[6:8, :] = jnp.zeros((2, width), F32)
    rows.send()


def feed_back(codes, residual, own_wide, wide, tangent, expander, gain, combiner):
    rows, width = residual.shape
    return staged(
        feed_back_body,
        [home(residual), ready(tangent), ready(expander), gain, ready(combiner), apart(own_wide), apart(wide)],
        [((rows, width), F32), ((rows, width), BF)] + [((rows, MINE), BF)] * 4 + [((8, width), F32)],
        name="feed_back",
        mib=24,
        scratch=[pltpu.VMEM(wide.shape, BF), pltpu.SemaphoreType.DMA((1,))],
        code=codes,
    )


def outcome_body(code, ins, outs, active_ref, sem):
    residual, squeezer, leveling, own_wide, wide = ins

    for core, source in enumerate((own_wide, wide)):

        @pl.when(code[3] == core)
        def _():
            pltpu.make_async_copy(source(), active_ref, sem.at[0]).start()

    pltpu.make_async_copy(wide(), active_ref, sem.at[0]).wait()
    outs[0].ref[...] = (residual()[...] + dot(active_ref[...], squeezer()[...]) + leveling()[...]).astype(BF)
    outs[0].send()


def outcome_of(codes, residual, own_wide, wide, squeezer, leveling):
    rows, width = residual.shape
    return staged(
        outcome_body,
        [home(residual), ready(squeezer), leveling, apart(own_wide), apart(wide)],
        [((rows, width), BF)],
        name="outcome",
        mib=16,
        scratch=[pltpu.VMEM(wide.shape, BF), pltpu.SemaphoreType.DMA((1,))],
        code=codes,
    )[0]


PARTS = 16


def place(code, piece, size):
    return pl.multiple_of((piece ^ code) * size, 8)


def segments(first, rows, low, size):
    out, at = [], first
    while at < first + rows:
        piece, offset = divmod(at - low, size)
        count = min(size - offset, first + rows - at)
        out.append((piece, offset, at - first, count))
        at += count
    return out


def spread(hold_ref, block, first, low, size, code):
    for piece, offset, start, count in segments(first, block.shape[0], low, size):
        at = pl.multiple_of(place(code, piece, size) + offset, 8)
        hold_ref[pl.ds(at, count), :] = block[start : start + count]


def feed_grad_body(sizes, code, ins, outs, *holds):
    own_wide, own_slim, wide, slim, own, far, near, rest, resid, other = ins
    hid, width = own_wide().shape[1], own_slim().shape[1]
    bulk = PARTS * sizes[0]
    refs = [arrival() for arrival in (own_wide, own_slim, wide, slim)]

    def put(block, row):
        for part, low, high in ((0, 0, bulk), (1, bulk, bulk + PARTS * sizes[1])):
            first, last = max(row, low), min(row + block.shape[0], high)
            if first < last:
                spread(holds[part], block[first - row : last - row], first, low, sizes[part], code[4 + 2 * part])

    for j in range(hid // width):
        cut = slice(j * width, (j + 1) * width)
        for one in range(2):

            @pl.when(code[3] == one)
            def _():
                if one:
                    block = tdot(refs[1][...], refs[0][:, cut]) + tdot(refs[3][...], refs[2][:, cut])
                else:
                    block = tdot(refs[0][:, cut], refs[1][...]) + tdot(refs[2][:, cut], refs[3][...])
                put(block, j * width)

    upper = code[2] < 2
    for i in range(2):
        here = jnp.where(upper, (own, far)[i]()[...], (far, own)[i]()[...])
        peer = jnp.where(upper, (near, rest)[i]()[...], (rest, near)[i]()[...])
        put(tdot(here, resid()[...]) + tdot(peer, other()[...]), hid + i * MINE)
    for part, hold_ref in enumerate(holds):
        keep, send = outs[2 * part : 2 * part + 2]
        half = hold_ref.shape[0] // 2
        send.ref[...] = hold_ref[half:, :].astype(BF)
        send.send()
        keep.ref[...] = hold_ref[:half, :].astype(BF)
        keep.send()


def feed_grad(codes, sizes, feed, mixed):
    width = feed[1].shape[1]
    halves = [((PARTS * size // 2, width), BF) for size in sizes]
    return staged(
        functools.partial(feed_grad_body, sizes),
        [home(feed[0]), home(feed[1]), *feed[2:], *mixed],
        [halves[0], halves[0], halves[1], halves[1]],
        name="feed_grad",
        mib=40,
        scratch=[pltpu.VMEM((PARTS * size, width), F32) for size in sizes],
        code=codes,
    )


def feed_assemble_body(sizes, code, ins, outs, *holds):
    squeezer, expander, combiner = outs
    hid, width = squeezer.target.shape
    sems, moves = squeezer.sems, squeezer.moves

    def targets(core, row, count):
        out = []
        while count:
            if row < hid and core == 0:
                take = min(count, hid - row)
                out.append((squeezer.target.at[pl.ds(row, take), :], take))
            elif row < hid:
                j = row // width
                take = min(count, (j + 1) * width - row)
                cut = pl.ds(row - j * width, take), pl.ds(j * width, width)
                out.append((expander.target.at[cut], take))
            else:
                view, at = divmod(row - hid, MINE)
                take = min(count, MINE - at)
                out.append((combiner.target.at[pl.ds((core + 2 * view) * MINE + at, take), :], take))
            row, count = row + take, count - take
        return out

    def copies(me):
        out = []
        for side in range(2):
            core = me if side == 0 else 1 - me
            low = 0
            for part, size in enumerate(sizes):
                code_here = code[4 + 2 * part + side]
                for piece in range(PARTS):
                    at = 0
                    for target, count in targets(core, low + piece * size, size):
                        start = pl.multiple_of(place(code_here, piece, size) + at, 8)
                        source = holds[2 * side + part].at[pl.ds(start, count), :]
                        out.append(pltpu.make_async_copy(source, target, sems.at[len(out)]))
                        at += count
                low += PARTS * size
        return out

    for i, hold_ref in enumerate(holds):
        half = hold_ref.shape[0] // 2
        hold_ref[:half, :] = ins[2 * i]()[...].astype(F32)
        hold_ref[half:, :] = ins[2 * i + 1]()[...].astype(F32)
    for me in range(2):

        @pl.when(code[3] == me)
        def _():
            here = copies(me)
            for move in here:
                move.start()
            for move in here:
                move.wait()


def feed_assemble(codes, blocks, hid, width):
    sizes = [blocks[0].shape[0] // 8, blocks[2].shape[0] // 8]

    def kernel(code_ref, *refs):
        ins, targets, bufs, rest = refs[:8], refs[8:11], refs[11:19], refs[19:]
        in_sems, out_sems, holds = rest[0], rest[1], rest[2:]
        arrivals = [Incoming(s, b, in_sems.at[i]) for i, (s, b) in enumerate(zip(ins, bufs, strict=True))]
        outs = [Outgoing(t, None, out_sems, []) for t in targets]
        feed_assemble_body(sizes, code_ref, arrivals, outs, *holds)

    anywhere = pl.BlockSpec(memory_space=pl.ANY)
    return pl.pallas_call(
        kernel,
        in_specs=[pl.BlockSpec(memory_space=pltpu.SMEM)] + [anywhere] * 8,
        out_specs=[anywhere] * 3,
        out_shape=[pltpu.HBM(s, F32) for s in ((hid, width), (width, hid), (width, width))],
        scratch_shapes=[pltpu.VMEM(b.shape, BF) for b in blocks]
        + [pltpu.SemaphoreType.DMA((8,)), pltpu.SemaphoreType.DMA((96,))]
        + [pltpu.VMEM((PARTS * size, width), F32) for size in sizes + sizes],
        compiler_params=pltpu.CompilerParams(vmem_limit_bytes=40 * MIB),
        cost_estimate=pl.CostEstimate(flops=0, bytes_accessed=0, transcendentals=0),
        name="feed_assemble",
    )(codes, *[pltpu.with_memory_space_constraint(b, pltpu.HBM) for b in blocks])


def input_grad_body(_, ins, outs, hold_ref):
    dqk, dv, weight, unit, rstd, gain, *rest = ins
    cams, resid = rest[:4], rest[4]
    small = outs[4]
    patches = resid.buffer.shape[0]
    groups = small.ref.shape[0] - 2
    slope = dott(dqk()[:, :MINE], weight()[:, :MINE]) + dott(dqk()[:, MINE:], weight()[:, PAD : PAD + MINE])
    slope += dott(dv()[...], weight()[:, 2 * PAD : 2 * PAD + MINE])
    values = unit()[...].astype(F32)
    small.ref[groups : groups + 1, :] = jnp.sum(slope * values, 0, keepdims=True)
    small.ref[groups + 1 : groups + 2, :] = jnp.sum(slope, 0, keepdims=True)
    hold_ref[...] = norm_back(slope * gain()[...], values, rstd()[...])
    table = jnp.zeros((groups, slope.shape[1]), F32)
    for r in (1, 3, 0, 2):
        part = hold_ref[r * patches : (r + 1) * patches, :]
        outs[r].ref[...] = part.astype(outs[r].ref.dtype)
        outs[r].send()
        if r == 0:
            part = part + resid()[...]
        hot = onehot_t(cams[r]()[...], groups)
        for piece in split3(part):
            table += dot(hot, piece)
    small.ref[:groups, :] = table
    small.send()


def input_grad(dqk, dv, weight, unit, rstd, gain, cams, resid, groups):
    total, width = unit.shape
    patches = resid.shape[0]
    low, full = ((patches, width), BF), ((patches, width), F32)
    return staged(
        input_grad_body,
        [home(dqk), home(dv), home(weight), home(unit), home(rstd), gain, *cams, home(resid)],
        [full, low, full, low, ((groups + 2, width), F32)],
        name="input_grad",
        mib=48,
        scratch=[pltpu.VMEM((total, width), F32)],
    )


def assemble_kernel(code_ref, a_ref, b_ref, c_ref, d_ref, out_ref):
    me = code_ref[2]
    rows = out_ref.shape[0]
    width = out_ref.shape[1] // 3
    blocks = [r[...].astype(F32) for r in (a_ref, b_ref, c_ref, d_ref)]
    for v, block in enumerate(by_view(blocks, me)):
        at = v * MINE
        out_ref[:, at : at + MINE] = block[:rows, :MINE]
        out_ref[:, width + at : width + at + MINE] = block[:rows, MINE:]
        out_ref[: rows // 2, 2 * width + at : 2 * width + at + MINE] = block[rows:, :MINE]
        out_ref[rows // 2 :, 2 * width + at : 2 * width + at + MINE] = block[rows:, MINE:]


def assemble(codes, blocks, width):
    rows = width // PIECES
    piece = rows * 3 // 2

    def part(which, far):
        def place(p, code):
            r = p ^ code[which]
            return ((r // 2 * 2 + far) * 2 + r % 2, 0)

        return pl.BlockSpec((piece, 2 * MINE), place)

    own, near = blocks
    return pl.pallas_call(
        assemble_kernel,
        grid_spec=pltpu.PrefetchScalarGridSpec(
            num_scalar_prefetch=1,
            grid=(PIECES,),
            in_specs=[part(0, 0), part(1, 0), part(0, 1), part(1, 1)],
            out_specs=pl.BlockSpec((rows, 3 * width), lambda p, code: (p, 0)),
        ),
        out_shape=jax.ShapeDtypeStruct((width, 3 * width), F32),
        compiler_params=pltpu.CompilerParams(vmem_limit_bytes=24 * MIB),
        cost_estimate=pl.CostEstimate(flops=0, bytes_accessed=0, transcendentals=0),
        name="assemble",
    )(codes, own, near, own, near)


def small_kernel(here_ref, there_ref, table_ref, *refs):
    groups, width = table_ref.shape
    total = here_ref[...].astype(F32) + there_ref[...].astype(F32)
    table_ref[...] = total[:groups, :]
    row = groups
    for ref in refs:
        for at in range(0, ref.shape[0], width):
            ref[at : at + width] = total[row, :]
            row += 1


def small_outputs(here, there, groups, sizes):
    shapes = [(groups, here.shape[1])] + [(n,) for n in sizes]
    return pl.pallas_call(
        small_kernel,
        out_shape=[jax.ShapeDtypeStruct(s, F32) for s in shapes],
        cost_estimate=pl.CostEstimate(flops=0, bytes_accessed=0, transcendentals=0),
        name="small_outputs",
    )(here, there)


def after(values, *others):
    out = lax.optimization_barrier((*values, *others))
    return out[: len(values)]


def on_device(
    inputs,
    cameras,
    embedding,
    scaling,
    shifting,
    projector,
    combiner,
    baseline,
    rescaling,
    reshifting,
    expander,
    priming,
    squeezer,
    leveling,
    cotangent,
):
    me = lax.axis_index("view")
    core = me % 2
    patches, width = inputs.shape[2], inputs.shape[3]
    groups, hid = embedding.shape[0], expander.shape[1]
    codes = [code_of(SCENE, core), code_of(SCENE, 1 - core), me, core]
    codes += [code_of(WIDE, core), code_of(WIDE, 1 - core), code_of(THIN, core), code_of(THIN, core)]
    codes = jnp.stack(codes).astype(jnp.int32)
    tangent = cotangent.reshape(patches, width)
    x0 = inputs.reshape(patches, width)
    c0 = cameras.reshape(1, patches)
    x2, c2 = swap(x0, "view", 2), swap(c0, "view", 2)
    x1, c1 = swap(x0, "view", 1), swap(c0, "view", 1)
    hole = jnp.zeros((width, PAD - MINE), BF)
    padded = []
    for part in range(3):
        padded += [lax.dynamic_slice_in_dim(projector, part * width + me * MINE, MINE, 1), hole]
    padded = jnp.concatenate(padded, 1)
    *held, summed = project(x0, x1, c0, c1, embedding, scaling, shifting, padded)
    x2, c2 = after((x2, c2), *held)
    x3, c3 = swap(x2, "view", 1), swap(c2, "view", 1)
    normed, unit1, rstd1, q, k, v, e1, far, rest, mix1, inv1 = second_half(
        x2, x3, c2, c3, embedding, scaling, shifting, padded, held
    )
    far, rest = swap(far, "view", 2), swap(rest, "view", 3)
    e0, own, near, mix0, inv0 = attend(q, k, v)
    near, own, far, rest = after((near, own, far, rest))
    near, peer_rest = swap(near, "view", 1), swap(rest, "view", 1)

    residual, own_wide, wide, own_slim, slim = feed_forward(
        codes, summed, own, near, far, rest, combiner, baseline, rescaling, reshifting, expander, priming,
        squeezer, tangent,
    )
    peer_near = swap(near, "view", 1)
    peer_wide, peer_slim = swap(wide, "view", 1), swap(slim, "view", 1)
    residual_grad, resid_low, *grads, rows = feed_back(
        codes, residual, own_wide, wide, tangent, expander, rescaling, combiner
    )
    grads = [grads[0]] + [swap(grads[r], "view", r) for r in (1, 2, 3)]
    other = swap(resid_low, "view", 1)
    outcome = outcome_of(codes, residual, own_wide, wide, squeezer, leveling)
    other, peer_wide, peer_slim, peer_near, peer_rest, outcome = after(
        (other, peer_wide, peer_slim, peer_near, peer_rest, outcome)
    )
    sizes = [(hid + width // 2) // 24, (hid + width // 2) // 48]
    keep0, send0, keep1, send1 = feed_grad(
        codes, sizes, [own_wide, own_slim, peer_wide, peer_slim],
        [own, far, peer_near, peer_rest, resid_low, other],
    )
    *grads, keep0, send0, keep1, send1 = after((*grads, keep0, send0, keep1, send1))
    got0, got1 = swap_by_core(send0, WIDE[0]), swap_by_core(send1, THIN[0])
    dqk, dv, keep, send = attend_back(codes, q, k, v, e0, e1, grads, mix0, mix1, inv0, inv1, normed)
    got0, got1, dqk, dv, keep, send = after((got0, got1, dqk, dv, keep, send))

    def split(keep, got):
        cut = keep.shape[0] // 2
        return keep[:cut] + got[:cut], keep[cut:] + got[cut:]

    got = swap_by_core(send, SCENE[0])
    keep0, send0 = split(keep0, got0)
    keep1, send1 = split(keep1, got1)
    got0, got1 = swap_by_core(send0, WIDE[1]), swap_by_core(send1, THIN[1])
    own, near, far, rest, small = input_grad(
        dqk, dv, padded, unit1, rstd1, scaling, (c0, c1, c2, c3), residual_grad, groups
    )
    got, got0, got1, own, near, far, rest, small = after((got, got0, got1, own, near, far, rest, small))
    near, rest = swap(near, "view", 1), swap(rest, "view", 1)
    keep0, send0 = split(keep0, got0)
    keep1, send1 = split(keep1, got1)
    got0, got1 = swap_by_core(send0, WIDE[2]), swap_by_core(send1, THIN[2])
    keep, send = split(keep, got)
    got = swap_by_core(send, SCENE[1])
    small = rounded(jnp.concatenate([small, rows[:6]], 0)).reshape(-1, 2 * MINE)
    small = whole_slice(small)
    got0, got1, near, rest, small = after((got0, got1, near, rest, small))
    keep0, send0 = split(keep0, got0)
    keep1, send1 = split(keep1, got1)
    joint = jnp.concatenate([keep0, keep1], 0)
    got0 = swap_by_core(jnp.concatenate([send0, send1], 0), WIDE[3])
    far = swap((far + rest.astype(F32)).astype(BF), "view", 2)
    got, got0 = after((got, got0))
    keep, send = split(keep, got)
    got = swap_by_core(send, SCENE[2])
    joint = lax.optimization_barrier(whole_slice(joint + got0))
    got0 = swap_by_core(joint, WIDE[3])
    got, got0 = after((got, got0))
    keep = lax.optimization_barrier(whole_slice(keep + got))
    extra = small.shape[0]

    def grow(keep, small, got):
        small = rounded(small.astype(F32) + got[-extra:].astype(F32))
        return jnp.concatenate([keep, got[:-extra]], 0), small

    got = swap_by_core(jnp.concatenate([keep, small], 0), SCENE[2])
    all0 = jnp.concatenate([joint[: sizes[0]], got0[: sizes[0]]], 0)
    all1 = jnp.concatenate([joint[sizes[0] :], got0[sizes[0] :]], 0)
    got0, got1 = swap_by_core(all0, WIDE[2]), swap_by_core(all1, THIN[2])
    got, got0, got1 = after((got, got0, got1))
    all0, all1 = jnp.concatenate([all0, got0], 0), jnp.concatenate([all1, got1], 0)
    got0, got1 = swap_by_core(all0, WIDE[1]), swap_by_core(all1, THIN[1])
    keep, small = grow(keep, small, got)
    got = swap_by_core(jnp.concatenate([keep, small], 0), (Y, Y))
    inputs_grad = residual_grad + own + near.astype(F32) + far.astype(F32)
    got, got0, got1, inputs_grad = after((got, got0, got1, inputs_grad.astype(BF)))
    all0, all1 = jnp.concatenate([all0, got0], 0), jnp.concatenate([all1, got1], 0)
    got0, got1 = swap_by_core(all0, WIDE[0]), swap_by_core(all1, THIN[0])
    peer0, peer1 = swap(all0, "view", 1), swap(all1, "view", 1)
    keep, small = grow(keep, small, got)
    got = swap_by_core(jnp.concatenate([keep, small], 0), SCENE[1])
    got, peer0, peer1 = after((got, peer0, peer1))
    keep, small = grow(keep, small, got)
    got = swap_by_core(jnp.concatenate([keep, small], 0), SCENE[0])
    got0, got1, got = after((got0, got1, got))
    blocks = [all0, got0, all1, got1, peer0, swap(got0, "view", 1), peer1, swap(got1, "view", 1)]
    keep, small = grow(keep, small, got)
    near, other = swap(keep, "view", 1), swap(small, "view", 1)
    grad_squeezer, grad_expander, grad_combiner = feed_assemble(codes, blocks, hid, width)
    grad_projector = assemble(codes, [keep, near], width)
    vectors = [width] * 6 + [hid]
    table, *vectors = small_outputs(
        small.reshape(-1, width), other.reshape(-1, width), groups, vectors
    )
    grad_scaling, grad_shifting, grad_leveling, grad_baseline, grad_rescaling, grad_reshifting, grad_priming = vectors

    return (
        outcome.reshape(inputs.shape),
        inputs_grad.reshape(inputs.shape),
        table,
        grad_scaling,
        grad_shifting,
        grad_projector,
        grad_combiner,
        grad_baseline,
        grad_rescaling,
        grad_reshifting,
        grad_expander,
        grad_priming,
        grad_squeezer,
        grad_leveling,
    )


def solution(mesh):
    tokens = P("scene", "view", None, None)
    placed = (tokens, P("scene", "view", None)) + (P(),) * 12 + (tokens,)
    return jax.shard_map(
        on_device,
        mesh=mesh,
        in_specs=placed,
        out_specs=(tokens, tokens) + (P(),) * 12,
        check_vma=False,
    )
```

time: 431 us -> 247 us (0.57)
  local copies, waits for them, and re-layouts: 130 us -> 22.6 us
  Pallas kernels: 0 us -> 103 us
  matrix products: 89.6 us -> 0 us
  other arithmetic: 58.6 us -> 2.65 us
  waiting for transfers between devices: 112 us -> 70.8 us
  starting transfers between devices: 32.1 us -> 41.6 us
    pallas_call x0 -> x12, Pallas kernels: none -> 103 us  [the longest x9 88 us: staged(): pl.pallas_call(kernel, in_specs=specs, out_specs=[anywhere] * n_out, out_...]
    dot_general x20 -> x0, matrix products: 79.7 us -> none  [the longest x1 14.3 us: on_device(): jnp.einsum('qhd,khd->hqk', grad_out, v, preferred_element_type=F32)]
    slice x12 -> x4, local copies, waits for them, and re-layouts: 39.3 us -> 0.03 us  [the longest x2 0.02 us: on_device(): all0 = jnp.concatenate([joint[:sizes[0]], got0[:sizes[0]]], 0)]
    ppermute x15 -> x26, waiting for transfers between devices: 49.8 us -> 11.9 us  [swap(): return lax.ppermute(value, axis, [(i, i ^ mask) for i in range(count)])]
    concatenate x5 -> x3, local copies, waits for them, and re-layouts: 32.8 us -> 2.53 us  [the longest x1 2.34 us: on_device(): padded = jnp.concatenate(padded, 1)]
    convert_element_type x12 -> x7, other arithmetic: 20.7 us -> 1.86 us  [the longest x1 1.05 us: on_device(): inputs_grad.astype(BF)]
    select_n x12 -> x0, other arithmetic: 15.5 us -> none  [the longest x10 13.2 us: all_gather(): jnp.where(side == 0, value, got)]
    sub x1 -> x0, matrix products: 9.95 us -> none  [on_device(): expo = jnp.exp(scores - top)]
  transfers between devices with their start and end apart: 33 -> 47, of which waited for: 15 -> 16; matrix products, arithmetic and copies ran while one was open for 43% -> 6% of each run, Pallas kernels for 0% -> 33%
where the time goes in v2:
time: 247 us; the launch traced here: 243 us
  Pallas kernels  103 us (42%)
  waiting for transfers between devices  70.8 us (29%)
  starting transfers between devices  41.6 us (17%)
  local copies, waits for them, and re-layouts  22.6 us (9%)
  other arithmetic  2.65 us (1%)
    pallas_call x9, Pallas kernels, staged(): pl.pallas_call(kernel, in_specs=specs, out_specs=[anywhere] * n_out, out_...  88 us
    ppermute x21, waiting for transfers between devices, swap_by_core(): return lax.ppermute(value, BOTH, pairs)  58.9 us
    ppermute x21, starting transfers between devices, swap_by_core(): return lax.ppermute(value, BOTH, pairs)  27.4 us
    unnamed x98, local copies, waits for them, and re-layouts  14.3 us
    ppermute x26, starting transfers between devices, swap(): return lax.ppermute(value, axis, [(i, i ^ mask) for i in range(count)])  14.2 us
    ppermute x26, waiting for transfers between devices, swap(): return lax.ppermute(value, axis, [(i, i ^ mask) for i in range(count)])  11.9 us
    pallas_call x1, Pallas kernels, feed_assemble(): pl.pallas_call(kernel, in_specs=[pl.BlockSpec(memory_space=pltpu.SMEM)] +...  8.4 us
    pallas_call x1, Pallas kernels, assemble(): pl.pallas_call(assemble_kernel, grid_spec=pltpu.PrefetchScalarGridSpec(nu...  5.41 us
  transfers between devices with their start and end apart: 47, of which 16 were waited for; matrix products, arithmetic and copies ran while one was open for 6% of the time, Pallas kernels for 33%

profile of v2, /device:TPU:0, one launch (start us, length us, event | category | flops | bytes accessed | tf_op | source)
XLA Modules:
  0.0 243.0 jit_solution(439666183819473607)
XLA Ops:
  1.2 2.6 %collective-permute-start.2 = (bf16[328,768]{1,0:T(8,128)(2,1)}, bf16[328,768]{1,0:T(8,128)(2,1)S(1)}, u32[]{:S(2)}, u32[]{:S(2)}) collective-permute-start(bf16[328,768]{1,0:T(8,128)(2,1)} %bitcast.16), channel_id=1, source_target_pairs={{0,2},{1,3},{2,0},{3,1},{4,6},{5,7},{6,4},{7,5},{8,10},{9,11},{10,... | collective-permute-start | bytes 1511432 | tf_op jit(solution)/shard_map/ppermute | solution.py:22
  3.9 2.8 %constant_dynamic-slice_fusion = (bf16[768,192]{1,0:T(8,128)(2,1)S(1)}, bf16[768,192]{1,0:T(8,128)(2,1)}, bf16[768,192]{1,0:T(8,128)(2,1)}) fusion(bf16[768,2304]{1,0:T(8,128)(2,1)} %param.20, s32[]{:T(128)S(6)} %select_n.65, s32[]{:T(128)S(6)} %select_n.63, s32[]{:T(128)S(6)} %select_n.64), kind=kLoop, calls=%fused_computation.46 | loop fusion | bytes 1769484 | tf_op jit(solution)/shard_map/dynamic_slice | solution.py:919
  6.8 2.3 concatenate.58.refs_7_.refs_2_
  9.3 5.6 %project.1 = (bf16[1312,768]{1,0:T(8,128)(2,1)}, bf16[1312,768]{1,0:T(8,128)(2,1)}, f32[1312,1]{1,0:T(8,128)}, bf16[1312,256]{1,0:T(8,128)(2,1)}, bf16[1312,256]...) custom-call(bf16[328,768]{1,0:T(8,128)(2,1)S(1)} %bitcast.17, ...), custom_call_target="tpu_custom_call" | custom-call | tf_op jit(solution)/shard_map/project/pallas_call | solution.py:209
  16.7 2.0 copy.39.refs_14_
  18.7 2.0 copy.40.refs_15_
  21.8 11.4 %second_half.1 = (bf16[1312,768]{1,0:T(8,128)(2,1)}, bf16[1312,768]{1,0:T(8,128)(2,1)}, f32[1312,1]{1,0:T(8,128)}, bf16[1312,256]{1,0:T(8,128)(2,1)}, bf16[1312,...) custom-call(bf16[328,768]{1,0:T(8,128)(2,1)S(1)} %copy-done.13, ...), custom_call_target="tpu_custom_call", output_to_operand_aliasing={{0}: (10, {}), {1}: (11, {}), {2}: (12, {}), {3}: (13, {}),... | custom-call | tf_op jit(solution)/shard_map/second_half/pallas_call | solution.py:209
  33.3 1.8 collective-permute-start.6
  35.1 9.1 %attend.1 = (bf16[3,1312,656]{2,1,0:T(8,128)(2,1)}, bf16[328,192]{1,0:T(8,128)(2,1)}, bf16[328,192]{1,0:T(8,128)(2,1)}, f32[656,192]{1,0:T(8,128)}, f32[656,192]{1,0:T(8,128)}) custom-call(bf16[1312,256]{1,0:T(8,128)(2,1)} %get-tuple-element.138.refs_0_.refs_1_, bf16[1312,256]{1,0:T(8,128)(2,1)} %get-tuple-element.139.refs_1_.refs_2_, ...), custom_call_target="tpu_custom_call" | custom-call | tf_op jit(solution)/shard_map/attend/pallas_call | solution.py:209
  54.8 7.3 %feed_forward.1 = (f32[328,768]{1,0:T(8,128)}, bf16[328,1536]{1,0:T(8,128)(2,1)}, bf16[328,1536]{1,0:T(8,128)(2,1)}, bf16[328,768]{1,0:T(8,128)(2,1)}, bf16[328,768]{1,0:T(8,128)(2,1)}) custom-call(s32[8]{0:T(128)S(1)} %stack.32.refs_0_.code_ref, f32[328,768]{1,0:T(8,128)} %get-tuple-element.129.refs_1_, bf16[328,192]{1,0:T(8,128)(2,1)S(1)} %copy-done.9, ...), custom_call_target="tpu_custom_call" | custom-call | tf_op jit(solution)/shard_map/feed_forward/pallas_call | solution.py:209
  62.7 6.5 %feed_back.1 = (f32[328,768]{1,0:T(8,128)}, bf16[328,768]{1,0:T(8,128)(2,1)}, bf16[328,192]{1,0:T(8,128)(2,1)}, bf16[328,192]{1,0:T(8,128)(2,1)}, bf16[328,192]{...) custom-call(s32[8]{0:T(128)S(1)} %stack.32.refs_0_.code_ref, f32[328,768]{1,0:T(8,128)} %get-tuple-element.149.refs_1_, ...), custom_call_target="tpu_custom_call" | custom-call | tf_op jit(solution)/shard_map/feed_back/pallas_call | solution.py:209
  73.9 4.3 %outcome.1 = bf16[328,768]{1,0:T(8,128)(2,1)} custom-call(s32[8]{0:T(128)S(1)} %stack.32.refs_0_.code_ref, f32[328,768]{1,0:T(8,128)} %get-tuple-element.149.refs_1_, bf16[1536,768]{1,0:T(8,128)(2,1)S(1)} %copy-done.1, f32[768]{0:T(1024)S(1)} %copy-done.33, bf16[328,1536]{1,0:T(8,128)(2,1)} %get-tuple-element.150.refs_6_.refs_4_.refs_1_, ...), custom_call_target="tpu_custom_call" | custom-call | tf_op jit(solution)/shard_map/outcome/pallas_call | solution.py:209
  78.3 8.7 %feed_grad.1 = (bf16[640,768]{1,0:T(8,128)(2,1)}, bf16[640,768]{1,0:T(8,128)(2,1)}, bf16[320,768]{1,0:T(8,128)(2,1)}, bf16[320,768]{1,0:T(8,128)(2,1)}) custom-call(s32[8]{0:T(128)S(1)} %stack.32.refs_0_.code_ref, bf16[328,1536]{1,0:T(8,128)(2,1)} %get-tuple-element.150.refs_6_.refs_4_.refs_1_, bf16[328,768]{1,0:T(8,128)(2,1)} %get-tuple-element.159.refs_2_, ...), custom_call_target="tpu_custom_call" | custom-call | tf_op jit(solution)/shard_map/feed_grad/pallas_call | solution.py:209
  90.1 24.5 %attend_back.1 = (bf16[1312,384]{1,0:T(8,128)(2,1)}, bf16[1312,192]{1,0:T(8,128)(2,1)}, bf16[576,384]{1,0:T(8,128)(2,1)}, bf16[576,384]{1,0:T(8,128)(2,1)}) custom-call(s32[8]{0:T(128)S(1)} %stack.32.refs_0_.code_ref, bf16[1312,256]{1,0:T(8,128)(2,1)} %get-tuple-element.138.refs_0_.refs_1_, bf16[1312,256]{1,0:T(8,128)(2,1)} %get-tuple-element.139.refs_1_.refs_2_, ...), custom_call_target="tpu_custom_call" | custom-call | tf_op jit(solution)/shard_map/attend_back/pallas_call | solution.py:209
  117.7 10.6 %input_grad.1 = (f32[328,768]{1,0:T(8,128)}, bf16[328,768]{1,0:T(8,128)(2,1)}, f32[328,768]{1,0:T(8,128)}, bf16[328,768]{1,0:T(8,128)(2,1)}, f32[18,768]{1,0:T(8,128)}) custom-call(bf16[1312,384]{1,0:T(8,128)(2,1)} %get-tuple-element.192.refs_0_, bf16[1312,192]{1,0:T(8,128)(2,1)} %get-tuple-element.193.refs_1_, bf16[768,768]{1,0:T(8,128)(2,1)} %copy-done, ...), custom_call_target="tpu_custom_call" | custom-call | tf_op jit(solution)/shard_map/input_grad/pallas_call | solution.py:209
  134.1 2.9 %collective-permute-done.23 = bf16[160,768]{1,0:T(8,128)(2,1)S(1)} collective-permute-done((bf16[160,768]{1,0:T(8,128)(2,1)S(1)}, bf16[160,768]{1,0:T(8,128)(2,1)S(1)}, u32[]{:S(2)}, u32[]{:S(2)}) %collective-permute-start.23) | collective-permute-done | bytes 245792 | tf_op jit(solution)/shard_map/ppermute | solution.py:32
  137.2 2.6 %collective-permute-start.27 = (bf16[120,768]{1,0:T(8,128)(2,1)S(1)}, bf16[120,768]{1,0:T(8,128)(2,1)S(1)}, u32[]{:S(2)}, u32[]{:S(2)}) collective-permute-start(bf16[120,768]{1,0:T(8,128)(2,1)S(1)} %pad_maximum_fusion.7), channel_id=1, source_target_pairs={{0,16},{1,17},{2,18},{3,19},{4,20},{5,21},{6,22},{7,23},{8,24},{9,... | collective-permute-start | bytes 552968 | tf_op jit(solution)/shard_map/ppermute | solution.py:32
  139.8 8.0 %collective-permute-done.27 = bf16[120,768]{1,0:T(8,128)(2,1)S(1)} collective-permute-done((bf16[120,768]{1,0:T(8,128)(2,1)S(1)}, bf16[120,768]{1,0:T(8,128)(2,1)S(1)}, u32[]{:S(2)}, u32[]{:S(2)}) %collective-permute-start.27) | collective-permute-done | bytes 184352 | tf_op jit(solution)/shard_map/ppermute | solution.py:32
  147.9 3.0 %collective-permute-start.28 = (bf16[144,384]{1,0:T(8,128)(2,1)S(1)}, bf16[144,384]{1,0:T(8,128)(2,1)S(1)}, u32[]{:S(2)}, u32[]{:S(2)}) collective-permute-start(bf16[144,384]{1,0:T(8,128)(2,1)S(1)} %slice_add_fusion.12), channel_id=1, source_target_pairs={{0,16},{1,17},{2,18},{3,19},{4,20},{5,21},{6,22},{7,23},{8,24},{9,... | collective-permute-start | bytes 331784 | tf_op jit(solution)/shard_map/ppermute | solution.py:32
  150.9 11.9 %collective-permute-done.28 = bf16[144,384]{1,0:T(8,128)(2,1)S(1)} collective-permute-done((bf16[144,384]{1,0:T(8,128)(2,1)S(1)}, bf16[144,384]{1,0:T(8,128)(2,1)S(1)}, u32[]{:S(2)}, u32[]{:S(2)}) %collective-permute-start.28) | collective-permute-done | bytes 110624 | tf_op jit(solution)/shard_map/ppermute | solution.py:32
  163.7 1.8 collective-permute-start.31
  165.6 1.9 collective-permute-start.36
  168.2 3.7 %collective-permute-done.30 = bf16[192,384]{1,0:T(8,128)(2,1)S(1)} collective-permute-done((bf16[192,384]{1,0:T(8,128)(2,1)S(1)}, bf16[192,384]{1,0:T(8,128)(2,1)S(1)}, u32[]{:S(2)}, u32[]{:S(2)}) %collective-permute-start.30) | collective-permute-done | bytes 147488 | tf_op jit(solution)/shard_map/ppermute | solution.py:32
  175.4 4.7 %collective-permute-done.36 = bf16[328,768]{1,0:T(8,128)(2,1)S(1)} collective-permute-done((bf16[328,768]{1,0:T(8,128)(2,1)S(1)}, bf16[328,768]{1,0:T(8,128)(2,1)S(1)}, u32[]{:S(2)}, u32[]{:S(2)}) %collective-permute-start.36) | collective-permute-done | bytes 503840 | tf_op jit(solution)/shard_map/ppermute | solution.py:22
  181.2 8.8 %collective-permute-done.33 = bf16[336,384]{1,0:T(8,128)(2,1)S(1)} collective-permute-done((bf16[336,384]{1,0:T(8,128)(2,1)S(1)}, bf16[336,384]{1,0:T(8,128)(2,1)S(1)}, u32[]{:S(2)}, u32[]{:S(2)}) %collective-permute-start.33) | collective-permute-done | bytes 258080 | tf_op jit(solution)/shard_map/ppermute | solution.py:32
  190.9 1.9 collective-permute-start.37
  194.5 9.8 %collective-permute-done.37 = bf16[624,384]{1,0:T(8,128)(2,1)S(1)} collective-permute-done((bf16[624,384]{1,0:T(8,128)(2,1)S(1)}, bf16[624,384]{1,0:T(8,128)(2,1)S(1)}, u32[]{:S(2)}, u32[]{:S(2)}) %collective-permute-start.37) | collective-permute-done | bytes 479264 | tf_op jit(solution)/shard_map/ppermute | solution.py:32
  204.6 2.3 collective-permute-start.42
  208.3 9.6 %collective-permute-done.41.refs_3_ = bf16[320,768]{1,0:T(8,128)(2,1)} collective-permute-done((bf16[320,768]{1,0:T(8,128)(2,1)S(1)}, bf16[320,768]{1,0:T(8,128)(2,1)}, u32[]{:S(2)}, u32[]{:S(2)}) %collective-permute-start.41) | collective-permute-done | bytes 491552 | tf_op jit(solution)/shard_map/ppermute | solution.py:32
  222.8 3.2 %collective-permute-done.43 = bf16[48,384]{1,0:T(8,128)(2,1)} collective-permute-done((bf16[48,384]{1,0:T(8,128)(2,1)}, bf16[48,384]{1,0:T(8,128)(2,1)}, u32[]{:S(2)}, u32[]{:S(2)}) %collective-permute-start.43) | collective-permute-done | bytes 36896 | tf_op jit(solution)/shard_map/ppermute | solution.py:22
  228.9 8.4 %feed_assemble.1 = (f32[1536,768]{1,0:T(8,128)}, f32[768,1536]{1,0:T(8,128)}, f32[768,768]{1,0:T(8,128)}) custom-call(s32[8]{0:T(128)S(1)} %stack.32.refs_0_.code_ref, bf16[640,768]{1,0:T(8,128)(2,1)} %copy-done.35, bf16[640,768]{1,0:T(8,128)(2,1)} %collective-permute-done.40.refs_1_, bf16[320,768]{1,0:T(8,128)(2,1)} %copy-done.36, ...), custom_call_target="tpu_custom_call" | custom-call | tf_op jit(solution)/shard_map/feed_assemble/pallas_call | solution.py:767
  237.3 5.4 %assemble.1 = f32[768,2304]{1,0:T(8,128)} custom-call(s32[8]{0:T(128)S(1)} %stack.32.refs_0_.code_ref, bf16[2304,384]{1,0:T(8,128)(2,1)S(1)} %slice_dynamic-update-slice_fusion.a_ref.c_ref, bf16[2304,384]{1,0:T(8,128)(2,1)S(1)} %collective-permute-done.44.b_ref.d_ref, bf16[2304,384]{1,0:T(8,128)(2,1)S(1)} %slice_dynamic-update-slice_fusion.a_ref.c_ref, ...), custom_call_target="tpu_custom_call" | custom-call | tf_op jit(solution)/shard_map/assemble/pallas_call | solution.py:846
  (212 shorter events, 49.6 us)
Async XLA Ops:
  0.6 8.6 %collective-permute-start = (bf16[328,768]{1,0:T(8,128)(2,1)}, bf16[328,768]{1,0:T(8,128)(2,1)S(1)}, u32[]{:S(2)}, u32[]{:S(2)}) collective-permute-start(bf16[328,768]{1,0:T(8,128)(2,1)} %bitcast.15), channel_id=1, source_target_pairs={{0,1},{1,0},{2,3},{3,2},{4,5},{5,4},{6,7},{7,6},{8,9},{9,8},{10,11... | collective-permute-start | bytes 1511432 | tf_op jit(solution)/shard_map/ppermute | solution.py:22
  1.2 14.9 %collective-permute-start.2 = (bf16[328,768]{1,0:T(8,128)(2,1)}, bf16[328,768]{1,0:T(8,128)(2,1)S(1)}, u32[]{:S(2)}, u32[]{:S(2)}) collective-permute-start(bf16[328,768]{1,0:T(8,128)(2,1)} %bitcast.16), channel_id=1, source_target_pairs={{0,2},{1,3},{2,0},{3,1},{4,6},{5,7},{6,4},{7,5},{8,10},{9,11},{10,... | collective-permute-start | bytes 1511432 | tf_op jit(solution)/shard_map/ppermute | solution.py:22
  3.8 12.3 %collective-permute-start.3 = (s32[1,328]{1,0:T(1,128)}, s32[1,328]{1,0:T(1,128)S(1)}, u32[]{:S(2)}, u32[]{:S(2)}) collective-permute-start(s32[1,328]{1,0:T(1,128)} %bitcast.18), channel_id=1, source_target_pairs={{0,2},{1,3},{2,0},{3,1},{4,6},{5,7},{6,4},{7,5},{8,10},{9,11},{10,... | collective-permute-start | bytes 3944 | tf_op jit(solution)/shard_map/ppermute | solution.py:22
  33.3 10.9 %collective-permute-start.6 = (bf16[328,192]{1,0:T(8,128)(2,1)}, bf16[328,192]{1,0:T(8,128)(2,1)S(1)}, u32[]{:S(2)}, u32[]{:S(2)}) collective-permute-start(bf16[328,192]{1,0:T(8,128)(2,1)} %get-tuple-element.143), channel_id=1, source_target_pairs={{0,2},{1,3},{2,0},{3,1},{4,6},{5,7},{6,4},{7,5},{8,10},{9,11},{10,... | collective-permute-start | bytes 377864 | tf_op jit(solution)/shard_map/ppermute | solution.py:22
  35.1 9.8 %collective-permute-start.7 = (bf16[328,192]{1,0:T(8,128)(2,1)}, bf16[328,192]{1,0:T(8,128)(2,1)S(1)}, u32[]{:S(2)}, u32[]{:S(2)}) collective-permute-start(bf16[328,192]{1,0:T(8,128)(2,1)} %get-tuple-element.144), channel_id=1, source_target_pairs={{0,3},{1,2},{2,1},{3,0},{4,7},{5,6},{6,5},{7,4},{8,11},{9,10},{10,... | collective-permute-start | bytes 377864 | tf_op jit(solution)/shard_map/ppermute | solution.py:22
  62.1 16.1 %collective-permute-start.10 = (bf16[328,1536]{1,0:T(8,128)(2,1)}, bf16[328,1536]{1,0:T(8,128)(2,1)S(1)}, u32[]{:S(2)}, u32[]{:S(2)}) collective-permute-start(bf16[328,1536]{1,0:T(8,128)(2,1)} %get-tuple-element.151.refs_7_.refs_5_), channel_id=1, source_target_pairs={{0,1},{1,0},{2,3},{3,2},{4,5},{5,4},{6,7},{7,6},{8,9},{9,8},{10,11... | collective-permute-start | bytes 3022856 | tf_op jit(solution)/shard_map/ppermute | solution.py:22
  62.6 11.3 %collective-permute-start.11 = (bf16[328,768]{1,0:T(8,128)(2,1)}, bf16[328,768]{1,0:T(8,128)(2,1)S(1)}, u32[]{:S(2)}, u32[]{:S(2)}) collective-permute-start(bf16[328,768]{1,0:T(8,128)(2,1)} %get-tuple-element.153), channel_id=1, source_target_pairs={{0,1},{1,0},{2,3},{3,2},{4,5},{5,4},{6,7},{7,6},{8,9},{9,8},{10,11... | collective-permute-start | bytes 1511432 | tf_op jit(solution)/shard_map/ppermute | solution.py:22
  69.3 9.0 %collective-permute-start.9 = (bf16[328,768]{1,0:T(8,128)(2,1)}, bf16[328,768]{1,0:T(8,128)(2,1)S(1)}, u32[]{:S(2)}, u32[]{:S(2)}) collective-permute-start(bf16[328,768]{1,0:T(8,128)(2,1)} %get-tuple-element.152.refs_9_), channel_id=1, source_target_pairs={{0,1},{1,0},{2,3},{3,2},{4,5},{5,4},{6,7},{7,6},{8,9},{9,8},{10,11... | collective-permute-start | bytes 1511432 | tf_op jit(solution)/shard_map/ppermute | solution.py:22
  71.7 15.3 %collective-permute-start.14 = (bf16[328,192]{1,0:T(8,128)(2,1)}, bf16[328,192]{1,0:T(8,128)(2,1)S(1)}, u32[]{:S(2)}, u32[]{:S(2)}) collective-permute-start(bf16[328,192]{1,0:T(8,128)(2,1)} %get-tuple-element.156), channel_id=1, source_target_pairs={{0,1},{1,0},{2,3},{3,2},{4,5},{5,4},{6,7},{7,6},{8,9},{9,8},{10,11... | collective-permute-start | bytes 377864 | tf_op jit(solution)/shard_map/ppermute | solution.py:22
  72.1 15.0 %collective-permute-start.15 = (bf16[328,192]{1,0:T(8,128)(2,1)}, bf16[328,192]{1,0:T(8,128)(2,1)S(1)}, u32[]{:S(2)}, u32[]{:S(2)}) collective-permute-start(bf16[328,192]{1,0:T(8,128)(2,1)} %get-tuple-element.157), channel_id=1, source_target_pairs={{0,2},{1,3},{2,0},{3,1},{4,6},{5,7},{6,4},{7,5},{8,10},{9,11},{10,... | collective-permute-start | bytes 377864 | tf_op jit(solution)/shard_map/ppermute | solution.py:22
  73.9 13.2 %collective-permute-start.16 = (bf16[328,192]{1,0:T(8,128)(2,1)}, bf16[328,192]{1,0:T(8,128)(2,1)S(1)}, u32[]{:S(2)}, u32[]{:S(2)}) collective-permute-start(bf16[328,192]{1,0:T(8,128)(2,1)} %get-tuple-element.158), channel_id=1, source_target_pairs={{0,3},{1,2},{2,1},{3,0},{4,7},{5,6},{6,5},{7,4},{8,11},{9,10},{10,... | collective-permute-start | bytes 377864 | tf_op jit(solution)/shard_map/ppermute | solution.py:22
  87.0 27.6 %collective-permute-start.17 = (bf16[640,768]{1,0:T(8,128)(2,1)}, bf16[640,768]{1,0:T(8,128)(2,1)S(1)}, u32[]{:S(2)}, u32[]{:S(2)}) collective-permute-start(bf16[640,768]{1,0:T(8,128)(2,1)} %get-tuple-element.169), channel_id=1, source_target_pairs={{0,4},{1,9},{2,6},{3,11},{4,0},{5,13},{6,2},{7,15},{8,12},{9,1},{1... | collective-permute-start | bytes 2949128 | tf_op jit(solution)/shard_map/ppermute | solution.py:32
  88.6 26.0 %collective-permute-start.18 = (bf16[320,768]{1,0:T(8,128)(2,1)}, bf16[320,768]{1,0:T(8,128)(2,1)S(1)}, u32[]{:S(2)}, u32[]{:S(2)}) collective-permute-start(bf16[320,768]{1,0:T(8,128)(2,1)} %get-tuple-element.170), channel_id=1, source_target_pairs={{0,2},{1,3},{2,0},{3,1},{4,6},{5,7},{6,4},{7,5},{8,10},{9,11},{10,... | collective-permute-start | bytes 1474568 | tf_op jit(solution)/shard_map/ppermute | solution.py:32
  114.7 13.7 %collective-permute-start.19 = (bf16[576,384]{1,0:T(8,128)(2,1)}, bf16[576,384]{1,0:T(8,128)(2,1)S(1)}, u32[]{:S(2)}, u32[]{:S(2)}) collective-permute-start(bf16[576,384]{1,0:T(8,128)(2,1)} %get-tuple-element.187), channel_id=1, source_target_pairs={{0,4},{1,9},{2,6},{3,11},{4,0},{5,13},{6,2},{7,15},{8,12},{9,1},{1... | collective-permute-start | bytes 1327112 | tf_op jit(solution)/shard_map/ppermute | solution.py:32
  115.4 13.2 %collective-permute-start.20 = (bf16[320,768]{1,0:T(8,128)(2,1)S(1)}, bf16[320,768]{1,0:T(8,128)(2,1)S(1)}, u32[]{:S(2)}, u32[]{:S(2)}) collective-permute-start(bf16[320,768]{1,0:T(8,128)(2,1)S(1)} %get-tuple-element.247), channel_id=1, source_target_pairs={{0,2},{1,5},{2,0},{3,7},{4,6},{5,1},{6,4},{7,3},{8,10},{9,13},{10,... | collective-permute-start | bytes 1474568 | tf_op jit(solution)/shard_map/ppermute | solution.py:32
  116.1 12.3 %collective-permute-start.21 = (bf16[160,768]{1,0:T(8,128)(2,1)S(1)}, bf16[160,768]{1,0:T(8,128)(2,1)S(1)}, u32[]{:S(2)}, u32[]{:S(2)}) collective-permute-start(bf16[160,768]{1,0:T(8,128)(2,1)S(1)} %get-tuple-element.252), channel_id=1, source_target_pairs={{0,8},{1,9},{2,10},{3,11},{4,12},{5,13},{6,14},{7,15},{8,0},{9,1},... | collective-permute-start | bytes 737288 | tf_op jit(solution)/shard_map/ppermute | solution.py:32
  137.2 10.6 %collective-permute-start.27 = (bf16[120,768]{1,0:T(8,128)(2,1)S(1)}, bf16[120,768]{1,0:T(8,128)(2,1)S(1)}, u32[]{:S(2)}, u32[]{:S(2)}) collective-permute-start(bf16[120,768]{1,0:T(8,128)(2,1)S(1)} %pad_maximum_fusion.7), channel_id=1, source_target_pairs={{0,16},{1,17},{2,18},{3,19},{4,20},{5,21},{6,22},{7,23},{8,24},{9,... | collective-permute-start | bytes 552968 | tf_op jit(solution)/shard_map/ppermute | solution.py:32
  147.8 15.0 %collective-permute-start.29 = (bf16[120,768]{1,0:T(8,128)(2,1)S(1)}, bf16[120,768]{1,0:T(8,128)(2,1)S(1)}, u32[]{:S(2)}, u32[]{:S(2)}) collective-permute-start(bf16[120,768]{1,0:T(8,128)(2,1)S(1)} %maximum_add_fusion), channel_id=1, source_target_pairs={{0,16},{1,17},{2,18},{3,19},{4,20},{5,21},{6,22},{7,23},{8,24},{9,... | collective-permute-start | bytes 552968 | tf_op jit(solution)/shard_map/ppermute | solution.py:32
  147.9 14.9 %collective-permute-start.28 = (bf16[144,384]{1,0:T(8,128)(2,1)S(1)}, bf16[144,384]{1,0:T(8,128)(2,1)S(1)}, u32[]{:S(2)}, u32[]{:S(2)}) collective-permute-start(bf16[144,384]{1,0:T(8,128)(2,1)S(1)} %slice_add_fusion.12), channel_id=1, source_target_pairs={{0,16},{1,17},{2,18},{3,19},{4,20},{5,21},{6,22},{7,23},{8,24},{9,... | collective-permute-start | bytes 331784 | tf_op jit(solution)/shard_map/ppermute | solution.py:32
  163.7 9.4 %collective-permute-start.31 = (bf16[160,768]{1,0:T(8,128)(2,1)S(1)}, bf16[160,768]{1,0:T(8,128)(2,1)S(1)}, u32[]{:S(2)}, u32[]{:S(2)}) collective-permute-start(bf16[160,768]{1,0:T(8,128)(2,1)S(1)} %pad_maximum_fusion.5), channel_id=1, source_target_pairs={{0,8},{1,3},{2,10},{3,1},{4,12},{5,7},{6,14},{7,5},{8,0},{9,11},{1... | collective-permute-start | bytes 737288 | tf_op jit(solution)/shard_map/ppermute | solution.py:32
  165.6 14.5 %collective-permute-start.36 = (bf16[328,768]{1,0:T(8,128)(2,1)S(1)}, bf16[328,768]{1,0:T(8,128)(2,1)S(1)}, u32[]{:S(2)}, u32[]{:S(2)}) collective-permute-start(bf16[328,768]{1,0:T(8,128)(2,1)S(1)} %add_convert_fusion.1), channel_id=1, source_target_pairs={{0,2},{1,3},{2,0},{3,1},{4,6},{5,7},{6,4},{7,5},{8,10},{9,11},{10,... | collective-permute-start | bytes 1511432 | tf_op jit(solution)/shard_map/ppermute | solution.py:22
  173.2 16.8 %collective-permute-start.34 = (bf16[320,768]{1,0:T(8,128)(2,1)S(1)}, bf16[320,768]{1,0:T(8,128)(2,1)S(1)}, u32[]{:S(2)}, u32[]{:S(2)}) collective-permute-start(bf16[320,768]{1,0:T(8,128)(2,1)S(1)} %pad_maximum_fusion.1), channel_id=1, source_target_pairs={{0,2},{1,5},{2,0},{3,7},{4,6},{5,1},{6,4},{7,3},{8,10},{9,13},{10,... | collective-permute-start | bytes 1474568 | tf_op jit(solution)/shard_map/ppermute | solution.py:32
  174.9 15.1 %collective-permute-start.33 = (bf16[336,384]{1,0:T(8,128)(2,1)S(1)}, bf16[336,384]{1,0:T(8,128)(2,1)S(1)}, u32[]{:S(2)}, u32[]{:S(2)}) collective-permute-start(bf16[336,384]{1,0:T(8,128)(2,1)S(1)} %pad_maximum_fusion.4), channel_id=1, source_target_pairs={{0,2},{1,3},{2,0},{3,1},{4,6},{5,7},{6,4},{7,5},{8,10},{9,11},{10,... | collective-permute-start | bytes 774152 | tf_op jit(solution)/shard_map/ppermute | solution.py:32
  190.1 14.3 %collective-permute-start.38 = (bf16[640,768]{1,0:T(8,128)(2,1)S(1)}, bf16[640,768]{1,0:T(8,128)(2,1)S(1)}, u32[]{:S(2)}, u32[]{:S(2)}) collective-permute-start(bf16[640,768]{1,0:T(8,128)(2,1)S(1)} %pad_maximum_fusion.refs_0_), channel_id=1, source_target_pairs={{0,1},{1,0},{2,3},{3,2},{4,5},{5,4},{6,7},{7,6},{8,9},{9,8},{10,11... | collective-permute-start | bytes 2949128 | tf_op jit(solution)/shard_map/ppermute | solution.py:22
  190.2 14.1 %collective-permute-start.39 = (bf16[320,768]{1,0:T(8,128)(2,1)S(1)}, bf16[320,768]{1,0:T(8,128)(2,1)S(1)}, u32[]{:S(2)}, u32[]{:S(2)}) collective-permute-start(bf16[320,768]{1,0:T(8,128)(2,1)S(1)} %pad_maximum_fusion.2.refs_2_), channel_id=1, source_target_pairs={{0,1},{1,0},{2,3},{3,2},{4,5},{5,4},{6,7},{7,6},{8,9},{9,8},{10,11... | collective-permute-start | bytes 1474568 | tf_op jit(solution)/shard_map/ppermute | solution.py:22
  190.9 13.4 %collective-permute-start.37 = (bf16[624,384]{1,0:T(8,128)(2,1)S(1)}, bf16[624,384]{1,0:T(8,128)(2,1)S(1)}, u32[]{:S(2)}, u32[]{:S(2)}) collective-permute-start(bf16[624,384]{1,0:T(8,128)(2,1)S(1)} %pad_maximum_fusion.3), channel_id=1, source_target_pairs={{0,8},{1,5},{2,10},{3,7},{4,12},{5,1},{6,14},{7,3},{8,0},{9,13},{1... | collective-permute-start | bytes 1437704 | tf_op jit(solution)/shard_map/ppermute | solution.py:32
  192.8 25.1 %collective-permute-start.40 = (bf16[640,768]{1,0:T(8,128)(2,1)S(1)}, bf16[640,768]{1,0:T(8,128)(2,1)}, u32[]{:S(2)}, u32[]{:S(2)}) collective-permute-start(bf16[640,768]{1,0:T(8,128)(2,1)S(1)} %pad_maximum_fusion.refs_0_), channel_id=1, source_target_pairs={{0,4},{1,9},{2,6},{3,11},{4,0},{5,13},{6,2},{7,15},{8,12},{9,1},{1... | collective-permute-start | bytes 2949128 | tf_op jit(solution)/shard_map/ppermute | solution.py:32
  204.6 14.6 %collective-permute-start.42 = (bf16[1200,384]{1,0:T(8,128)(2,1)S(1)}, bf16[1200,384]{1,0:T(8,128)(2,1)S(1)}, u32[]{:S(2)}, u32[]{:S(2)}) collective-permute-start(bf16[1200,384]{1,0:T(8,128)(2,1)S(1)} %constant_dynamic-update-slice_fusion), channel_id=1, source_target_pairs={{0,4},{1,9},{2,6},{3,11},{4,0},{5,13},{6,2},{7,15},{8,12},{9,1},{1... | collective-permute-start | bytes 2764808 | tf_op jit(solution)/shard_map/ppermute | solution.py:32
  206.8 11.1 %collective-permute-start.41 = (bf16[320,768]{1,0:T(8,128)(2,1)S(1)}, bf16[320,768]{1,0:T(8,128)(2,1)}, u32[]{:S(2)}, u32[]{:S(2)}) collective-permute-start(bf16[320,768]{1,0:T(8,128)(2,1)S(1)} %pad_maximum_fusion.2.refs_2_), channel_id=1, source_target_pairs={{0,2},{1,3},{2,0},{3,1},{4,6},{5,7},{6,4},{7,5},{8,10},{9,11},{10,... | collective-permute-start | bytes 1474568 | tf_op jit(solution)/shard_map/ppermute | solution.py:32
  219.4 17.9 %collective-permute-start.44 = (bf16[2304,384]{1,0:T(8,128)(2,1)S(1)}, bf16[2304,384]{1,0:T(8,128)(2,1)S(1)}, u32[]{:S(2)}, u32[]{:S(2)}) collective-permute-start(bf16[2304,384]{1,0:T(8,128)(2,1)S(1)} %slice_dynamic-update-slice_fusion.a_ref.c_ref), channel_id=1, source_target_pairs={{0,1},{1,0},{2,3},{3,2},{4,5},{5,4},{6,7},{7,6},{8,9},{9,8},{10,11... | collective-permute-start | bytes 5308424 | tf_op jit(solution)/shard_map/ppermute | solution.py:22
  220.2 8.7 %collective-permute-start.45 = (bf16[640,768]{1,0:T(8,128)(2,1)}, bf16[640,768]{1,0:T(8,128)(2,1)}, u32[]{:S(2)}, u32[]{:S(2)}) collective-permute-start(bf16[640,768]{1,0:T(8,128)(2,1)} %collective-permute-done.40.refs_1_), channel_id=1, source_target_pairs={{0,1},{1,0},{2,3},{3,2},{4,5},{5,4},{6,7},{7,6},{8,9},{9,8},{10,11... | collective-permute-start | bytes 2949128 | tf_op jit(solution)/shard_map/ppermute | solution.py:22
  220.3 8.6 %collective-permute-start.46 = (bf16[320,768]{1,0:T(8,128)(2,1)}, bf16[320,768]{1,0:T(8,128)(2,1)}, u32[]{:S(2)}, u32[]{:S(2)}) collective-permute-start(bf16[320,768]{1,0:T(8,128)(2,1)} %collective-permute-done.41.refs_3_), channel_id=1, source_target_pairs={{0,1},{1,0},{2,3},{3,2},{4,5},{5,4},{6,7},{7,6},{8,9},{9,8},{10,11... | collective-permute-start | bytes 1474568 | tf_op jit(solution)/shard_map/ppermute | solution.py:22
  (61 other events, 438.4 us)
